TPU v7x, 512 devices: a whole 4x8x8 slice. The times are simulated.
512 devices in a mesh: train: 32 (over z, y_hi, core), feat: 4 (over y_lo), query: 4 (over x).
Axes of the slice: x: 4, y: 8 (y_hi: 2, y_lo: 4; y = y_hi * 4 + y_lo), z: 8, core: 2. Of those that a mesh axis runs over, the one named last changes fastest.
Arguments:
- queries: bfloat16 [1536, 8192], P('query', 'train'), may hold values from -6 to 6
- precond: bfloat16 [8192, 8192], P('train', 'feat'), may hold values from -0.125 to 0.125
- train_feats: bfloat16 [28672, 8192], P('train', 'feat'), may hold values from -6 to 6
- query_cluster: int32 [1536], P('query'), may hold values from 0 to 15
- train_shard: int32 [28672], P('train'), may hold values from 0 to 63
- pairs: int32 [256, 2], replicated, may hold values from 0 to 63, as said below
- log_weight: int32 [28672], P('train'), may hold values from -8 to 8
Outputs:
- query_influence: float32 [1536], P('query')
- train_influence: float32 [28672], P('train')
Inputs may be any that keep to these rules, and one draw needn't show every extreme that they name: Rows are distinct pairs; the first entry is below 16, the second below 64.
All inputs are finite; a program needn't handle non-finite values.
Results may differ from a plain program's by a relative error of at most 0.0032.
Values may be sent and summed in bfloat16 or wider, within the bound.
No kernel may reach another device: no remote copies, remote signals or barrier semaphores. Data moves between devices by JAX's collectives and lax.ppermute only.
A program may use at most 64 MiB of HBM per device.

v0:
```python
import jax
import jax.numpy as jnp
from jax import lax
from jax.sharding import PartitionSpec as P

FEAT = 8192
CLUSTERS = 16
SHARDS = 64


def body(queries, precond, train_feats, query_cluster, train_shard, pairs, log_weight):
    highest = lax.Precision.HIGHEST
    query_rows = queries.shape[0]
    train_rows = train_feats.shape[0]
    scale = float(FEAT) ** (-0.5)
    pair_c = (pairs[:, 0][:, None] == jnp.arange(CLUSTERS, dtype=jnp.int32)[None, :]).astype(
        jnp.float32
    )
    pair_s = (pairs[:, 1][:, None] == jnp.arange(SHARDS, dtype=jnp.int32)[None, :]).astype(
        jnp.float32
    )
    active = jnp.dot(pair_c.T, pair_s, precision=highest)
    query_hot = (query_cluster[:, None] == jnp.arange(CLUSTERS, dtype=jnp.int32)[None, :]).astype(
        jnp.float32
    )
    query_mask = jnp.dot(query_hot, active, precision=highest)
    weight = jnp.exp2(log_weight.astype(jnp.float32) * 0.25)
    shard_hot = (train_shard[:, None] == jnp.arange(SHARDS, dtype=jnp.int32)[None, :]).astype(
        jnp.float32
    ) * weight[:, None]
    wmask = jnp.dot(query_mask, shard_hot.T, precision=highest)
    summed = lax.psum(jnp.dot(queries, precond, preferred_element_type=jnp.float32), "train")
    partial_value = lax.dot_general(
        summed.astype(jnp.bfloat16),
        train_feats,
        (((1,), (1,)), ((), ())),
        preferred_element_type=jnp.float32,
    )
    all_queries = float(query_rows * lax.axis_size("query")) ** (-0.5)
    all_samples = float(train_rows * lax.axis_size("train")) ** (-0.5)
    score = lax.psum(partial_value, "feat") * scale
    bounded = wmask * jnp.tanh(score)
    query_influence = lax.psum(jnp.sum(bounded, axis=1), "train") * all_samples
    train_influence = lax.psum(jnp.sum(bounded, axis=0), "query") * all_queries
    return (query_influence, train_influence)


def solution(mesh):
    return jax.shard_map(
        body,
        mesh=mesh,
        in_specs=(
            P("query", "train"),
            P("train", "feat"),
            P("train", "feat"),
            P("query"),
            P("train"),
            P(),
            P("train"),
        ),
        out_specs=(P("query"), P("train")),
        check_vma=False,
    )
```

profile of v0, /device:TPU:24, one launch (start us, length us, event | category | flops | bytes accessed | tf_op | source)
XLA Modules:
  0.0 440.2 jit_solution(337813107034344526)
XLA Ops:
  7.2 0.0 copy-start
  7.2 0.0 all-reduce.3.cloned.1.call-start
  7.2 1.2 copy-done
  8.4 3.2 fusion.14
  11.6 226.3 %all-reduce.4 = bf16[384,2048]{1,0:T(8,128)(2,1)S(1)} all-reduce(f32[384,2048]{1,0:T(8,128)} %fusion.14), channel_id=1, replica_groups=mesh['train'=32,'feat'=4,'query'=4] {'train'}, use_global_device_ids=true, to_apply=%region_0.0 | all-reduce | flops 786432 | bytes 4718592 | tf_op jit(solution)/shard_map/psum | solution.py:32
  237.9 0.0 copy-start.3
  237.9 0.0 copy-start.1
  237.9 0.0 copy-start.2
  237.9 5.0 %fusion.15 = f32[384,896]{1,0:T(8,128)} fusion(bf16[384,2048]{1,0:T(8,128)(2,1)S(1)} %all-reduce.4, bf16[896,2048]{1,0:T(8,128)(2,1)} %param.9), kind=kOutput, calls=%fused_computation.23 | convolution fusion | flops 1409286144 | bytes 6619136 | tf_op jit(solution)/shard_map/dot_general | solution.py:33
  242.9 0.0 copy-start.4
  242.9 0.0 all-reduce.3.cloned.1.call-update
  242.9 0.0 copy-done.3
  243.0 0.0 copy-done.1
  243.0 0.3 fusion.7
  243.3 0.0 copy-done.2
  243.3 0.3 fusion.6
  243.6 82.8 %all-reduce.3.cloned.1.call-done = f32[384,896]{1,0:T(8,128)} async-done(((f32[384,896]{1,0:T(8,128)}), f32[384,896]{1,0:T(8,128)}) %all-reduce.3.cloned.1.call-update) | async-done | bytes 1376272 | tf_op jit(solution)/shard_map/psum | solution.py:41
  326.4 0.0 copy-done.4
  326.4 2.9 fusion.12
  329.3 92.5 %psum.30 = f32[384]{0:T(512)S(1)} all-reduce(f32[384]{0:T(512)S(1)} %get-tuple-element.3), channel_id=1, replica_groups=mesh['train'=32,'feat'=4,'query'=4] {'train'}, use_global_device_ids=true, to_apply=%region_3.0 | all-reduce | flops 384 | bytes 3072 | tf_op jit(solution)/shard_map/psum | solution.py:43
  421.8 0.6 broadcast_multiply_fusion.1
  422.4 10.4 %psum.31 = f32[896]{0:T(1024)S(1)} all-reduce(f32[896]{0:T(1024)S(1)} %get-tuple-element.2), channel_id=1, replica_groups=mesh['train'=32,'feat'=4,'query'=4] {'query'}, use_global_device_ids=true, to_apply=%region_5.0 | all-reduce | flops 896 | bytes 7168 | tf_op jit(solution)/shard_map/psum | solution.py:44
  432.8 0.6 broadcast_multiply_fusion
  (2 shorter events, 0.0 us)
Async XLA Ops:
  7.2 1.2 copy-start
  7.2 319.2 %all-reduce.3.cloned.1.call-start = ((), (), s32[]{:S(2)}) async-start(), calls=%async_computation | async-start | bytes 2752512 | tf_op jit(solution)/shard_map/psum | solution.py:41
  237.9 5.0 %copy-start.3 = (s32[256,2]{0,1:T(2,128)S(1)}, s32[256,2]{0,1:T(2,128)}, u32[]{:S(2)}) copy-start(s32[256,2]{0,1:T(2,128)} %param.12) | copy-start | bytes 6148
  237.9 5.1 %copy-start.1 = (s32[896]{0:T(1024)S(1)}, s32[896]{0:T(1024)}, u32[]{:S(2)}) copy-start(s32[896]{0:T(1024)} %param.13) | copy-start | bytes 10756
  237.9 5.3 %copy-start.2 = (s32[384]{0:T(512)S(1)}, s32[384]{0:T(512)}, u32[]{:S(2)}) copy-start(s32[384]{0:T(512)} %param.10) | copy-start | bytes 4612
  242.9 83.5 %copy-start.4 = (s32[896]{0:T(1024)S(1)}, s32[896]{0:T(1024)}, u32[]{:S(2)}) copy-start(s32[896]{0:T(1024)} %param.11) | copy-start | bytes 10756
Sparse Core Ops, SparseCore 0:
  243.1 83.2 all-reduce.2
where the time goes:
time: 441 us; the launch traced here: 440 us
  blocking collectives  329 us (75%)
  waiting for transfers between devices  82.8 us (19%)
  between operations  14.1 us (3%)
  matrix products  11.6 us (3%)
    psum x1, blocking collectives, body(): lax.psum(jnp.dot(queries, precond, preferred_element_type=jnp.float32), '...  226 us
    psum x1, blocking collectives, body(): query_influence = lax.psum(jnp.sum(bounded, axis=1), 'train') * all_samples  92.5 us
    psum x1, waiting for transfers between devices, body(): score = lax.psum(partial_value, 'feat') * scale  82.8 us
    psum x1, blocking collectives, body(): train_influence = lax.psum(jnp.sum(bounded, axis=0), 'query') * all_queries  10.4 us
  transfers between devices with their start and end apart: 1, of which 1 were waited for; matrix products, arithmetic and copies ran while one was open for 0% of the time, Pallas kernels for 0%

commit v1 on v0

v1 whole, which is shorter than its diff:
```python
import jax
import jax.numpy as jnp
from jax import lax
from jax.sharding import Mesh, PartitionSpec as P

CLUSTERS = 16
SHARDS = 64
CORES = 2
Y_PARTS = 2
F32 = jnp.float32
BF16 = jnp.bfloat16
F16 = jnp.float16


def one_hot(ids, size):
    return (ids[:, None] == jnp.arange(size, dtype=jnp.int32)[None, :]).astype(BF16)


def other(x, axis, step=1):
    n = lax.axis_size(axis)
    return lax.ppermute(x, axis, [(i, i ^ step) for i in range(n)])


def to_all(x, axes, n):
    return lax.all_to_all(jnp.broadcast_to(x[None], (n,) + x.shape), axes, 0, 0)


def body(queries, precond, train_feats, query_cluster, train_shard, pairs, log_weight):
    n_z, n_f, n_q = lax.axis_size("z"), lax.axis_size("feat"), lax.axis_size("query")
    n_t = n_z * Y_PARTS
    core = lax.axis_index("c")
    lane = lax.axis_index("feat")
    query_rows, depth = queries.shape
    width = precond.shape[1]
    samples = train_feats.shape[0]
    feat = width * n_f
    half = query_rows // CORES
    rows = half // n_f

    mine = lax.dynamic_slice_in_dim(queries, core * half, half, 0)
    yours = lax.dynamic_slice_in_dim(queries, (1 - core) * half, half, 0)
    precond_other = other(precond, "c")
    theirs = other(yours, "c")
    part = jnp.dot(mine, precond, preferred_element_type=F32) + jnp.dot(
        theirs, precond_other, preferred_element_type=F32
    )
    up = 128.0
    pieces = (part * up).astype(F16).reshape(n_z, half // n_z, width)
    pieces, train_feats, train_shard, log_weight = lax.optimization_barrier(
        (pieces, train_feats, train_shard, log_weight)
    )
    feats_other = other(train_feats, "c")
    ids = jnp.stack([train_shard, log_weight])
    ids = jnp.concatenate([ids, other(ids, "c")], axis=1)
    pieces = lax.all_to_all(pieces, "z", 0, 0)
    block = jnp.sum(pieces.astype(F32), axis=0)
    sent = (block * (1.0 / n_z)).astype(F16)
    block = block * (1.0 / up) + other(sent, "yh").astype(F32) * (n_z / up)
    whole = lax.all_gather(block.astype(BF16), "z", axis=0, tiled=True)
    whole, feats_other = lax.optimization_barrier((whole, feats_other))

    dims = (((1,), (1,)), ((), ()))
    score = jnp.concatenate(
        [
            lax.dot_general(whole, train_feats, dims, preferred_element_type=F32).astype(BF16),
            lax.dot_general(whole, feats_other, dims, preferred_element_type=F32).astype(BF16),
        ],
        axis=1,
    )
    score = lax.all_to_all(score.reshape(n_f, rows, 2 * samples), "feat", 0, 0)
    score = jnp.sum(score.astype(F32), axis=0) * float(feat) ** (-0.5)

    active = jnp.minimum(
        lax.dot_general(
            one_hot(pairs[:, 0], CLUSTERS),
            one_hot(pairs[:, 1], SHARDS),
            (((0,), (0,)), ((), ())),
            preferred_element_type=F32,
        ),
        1.0,
    ).astype(BF16)
    clusters = lax.dynamic_slice_in_dim(query_cluster, core * half + lane * rows, rows, 0)
    query_mask = jnp.dot(one_hot(clusters, CLUSTERS), active, preferred_element_type=F32).astype(BF16)
    weight = jnp.exp2(ids[1].astype(F32) * 0.25)
    mask = lax.dot_general(query_mask, one_hot(ids[0], SHARDS), dims, preferred_element_type=F32)

    bounded = (mask * weight[None, :]) * jnp.tanh(score)
    by_query = jnp.sum(bounded, axis=1)
    by_sample = jnp.sum(bounded, axis=0)

    n_cf = CORES * n_f
    by_sample = by_sample.reshape(CORES, samples)
    by_sample = jnp.where(core == 0, by_sample, by_sample[::-1])
    both = jnp.concatenate([by_sample, jnp.broadcast_to(by_query[None], (CORES, rows))], axis=1)
    both = jnp.broadcast_to(both[None, :, None], (Y_PARTS, CORES, n_f, samples + rows))
    both = lax.all_to_all(both.reshape(Y_PARTS * n_cf, samples + rows), ("yh", "c", "feat"), 0, 0)
    both = both.reshape(Y_PARTS, n_cf, samples + rows)
    by_query = jnp.sum(both[:, :, samples:], axis=0).reshape(query_rows)
    by_sample = lax.dynamic_index_in_dim(both, lax.axis_index("yh"), 0, False)[:, :samples]
    by_sample = jnp.sum(by_sample, axis=0)

    both = to_all(jnp.concatenate([by_sample, by_query]), ("z", "query"), n_z * n_q)
    both = both.reshape(n_z, n_q, samples + query_rows)
    by_sample = lax.dynamic_index_in_dim(both, lax.axis_index("z"), 0, False)[:, :samples]
    by_query = lax.dynamic_index_in_dim(both, lax.axis_index("query"), 1, False)[:, samples:]
    by_sample = jnp.sum(by_sample, axis=0)
    by_query = jnp.sum(by_query, axis=0)
    all_queries = float(query_rows * n_q) ** (-0.5)
    all_samples = float(samples * n_t * CORES) ** (-0.5)
    return by_query * all_samples, by_sample * all_queries


def solution(mesh):
    n_train, n_feat, n_query = mesh.devices.shape
    fine = Mesh(
        mesh.devices.reshape(n_train // (Y_PARTS * CORES), Y_PARTS, CORES, n_feat, n_query),
        ("z", "yh", "c", "feat", "query"),
    )
    train = ("z", "yh", "c")
    return jax.shard_map(
        body,
        mesh=fine,
        in_specs=(
            P("query", train),
            P(train, "feat"),
            P(train, "feat"),
            P("query"),
            P(train),
            P(),
            P(train),
        ),
        out_specs=(P("query"), P(train)),
        check_vma=False,
    )
```

time: 441 us -> 137 us (0.31)
  the two profiles are of different devices: /device:TPU:24 before, /device:TPU:8 now
where the time goes in v1:
time: 137 us
  blocking collectives  59.7 us (44%)
  starting transfers between devices  36.1 us (26%)
  waiting for transfers between devices  28.6 us (21%)
  matrix products  5.71 us (4%)
  local copies, waits for them, and re-layouts  2.89 us (2%)
  other arithmetic  2.87 us (2%)
    all_to_all x1, blocking collectives, body(): pieces = lax.all_to_all(pieces, 'z', 0, 0)  33.9 us
    all_gather x1, blocking collectives, body(): whole = lax.all_gather(block.astype(BF16), 'z', axis=0, tiled=True)  25.8 us
    ppermute x5, starting transfers between devices, other(): return lax.ppermute(x, axis, [(i, i ^ step) for i in range(n)])  15.1 us
    all_to_all x1, waiting for transfers between devices, to_all(): return lax.all_to_all(jnp.broadcast_to(x[None], (n,) + x.shape), axes, 0, 0)  11.3 us
    all_to_all x1, starting transfers between devices, body(): lax.all_to_all(both.reshape(Y_PARTS * n_cf, samples + rows), ('yh', 'c',...  8.76 us
    all_to_all x1, waiting for transfers between devices, body(): lax.all_to_all(both.reshape(Y_PARTS * n_cf, samples + rows), ('yh', 'c',...  6.74 us
    all_to_all x1, starting transfers between devices, body(): score = lax.all_to_all(score.reshape(n_f, rows, 2 * samples), 'feat', 0, 0)  6.67 us
    all_to_all x1, waiting for transfers between devices, body(): score = lax.all_to_all(score.reshape(n_f, rows, 2 * samples), 'feat', 0, 0)  6.57 us
  transfers between devices with their start and end apart: 8, of which 5 were waited for; matrix products, arithmetic and copies ran while one was open for 2% of the time, Pallas kernels for 0%

profile of v1, /device:TPU:8, one launch (start us, length us, event | category | flops | bytes accessed | tf_op | source)
XLA Modules:
  0.0 136.9 jit_solution(6266467943444915148)
XLA Ops:
  0.6 0.0 copy-start
  0.6 2.1 %collective-permute-start.1 = (bf16[256,2048]{1,0:T(8,128)(2,1)}, bf16[256,2048]{1,0:T(8,128)(2,1)S(1)}, u32[]{:S(2)}, u32[]{:S(2)}) collective-permute-start(bf16[256,2048]{1,0:T(8,128)(2,1)} %param.8), channel_id=1, source_target_pairs={{0,16},{16,0},{1,17},{17,1},{2,18},{18,2},{3,19},{19,3},{4,20},{20... | collective-permute-start | bytes 3145736 | tf_op jit(solution)/shard_map/ppermute | solution.py:21
  2.7 0.0 copy-done
  2.7 2.4 %collective-permute-start = (bf16[192,256]{1,0:T(8,128)(2,1)S(1)}, bf16[192,256]{1,0:T(8,128)(2,1)S(1)}, u32[]{:S(2)}, u32[]{:S(2)}) collective-permute-start(bf16[192,256]{1,0:T(8,128)(2,1)S(1)} %constant_dynamic-slice_fusion.1), channel_id=1, source_target_pairs={{0,16},{16,0},{1,17},{17,1},{2,18},{18,2},{3,19},{19,3},{4,20},{20... | collective-permute-start | bytes 294920 | tf_op jit(solution)/shard_map/ppermute | solution.py:21
  5.2 0.0 copy-start.4
  5.2 1.8 %fusion.5 = f32[192,2048]{1,0:T(8,128)S(1)} fusion(bf16[256,2048]{1,0:T(8,128)(2,1)} %param.8, bf16[384,256]{1,0:T(8,128)(2,1)S(1)} %copy-done, s32[]{:T(128)S(6)} %select_n.31), kind=kOutput, calls=%fused_computation.19 | convolution fusion | flops 201326592 | bytes 2719748 | tf_op jit(solution)/shard_map/dot_general | solution.py:44
  6.9 0.0 collective-permute-done
  6.9 0.0 collective-permute-done.1
  7.0 0.4 fusion.1
  7.3 0.2 copy-done.4
  7.5 1.9 %collective-permute-start.4 = (bf16[896,2048]{1,0:T(8,128)(2,1)S(1)}, bf16[896,2048]{1,0:T(8,128)(2,1)S(1)}, u32[]{:S(2)}, u32[]{:S(2)}) collective-permute-start(bf16[896,2048]{1,0:T(8,128)(2,1)S(1)} %copy-done.4), channel_id=1, source_target_pairs={{0,16},{16,0},{1,17},{17,1},{2,18},{18,2},{3,19},{19,3},{4,20},{20... | collective-permute-start | bytes 11010056 | tf_op jit(solution)/shard_map/ppermute | solution.py:21
  9.4 33.9 %all_to_all.25 = f16[8,24,2048]{2,1,0:T(8,128)(2,1)S(1)} all-to-all(f16[8,24,2048]{2,1,0:T(8,128)(2,1)S(1)} %bitcast.22), channel_id=1, replica_groups=mesh['z'=8,'yh'=2,'c'=2,'feat'=4,'query'=4] {'z'}, dimensions={0} | all-to-all | bytes 1572864 | tf_op jit(solution)/shard_map/all_to_all | solution.py:55
  43.3 0.1 convert_reduce_fusion
  43.5 6.8 %collective-permute-start.3 = (f16[24,2048]{1,0:T(8,128)(2,1)S(1)}, f16[24,2048]{1,0:T(8,128)(2,1)S(1)}, u32[]{:S(2)}, u32[]{:S(2)}) collective-permute-start(f16[24,2048]{1,0:T(8,128)(2,1)S(1)} %multiply_convert_fusion), channel_id=1, source_target_pairs={{0,32},{32,0},{1,33},{33,1},{2,34},{34,2},{3,35},{35,3},{4,36},{36... | collective-permute-start | bytes 294920 | tf_op jit(solution)/shard_map/ppermute | solution.py:21
  50.3 3.8 %collective-permute-done.3 = f16[24,2048]{1,0:T(8,128)(2,1)S(1)} collective-permute-done((f16[24,2048]{1,0:T(8,128)(2,1)S(1)}, f16[24,2048]{1,0:T(8,128)(2,1)S(1)}, u32[]{:S(2)}, u32[]{:S(2)}) %collective-permute-start.3) | collective-permute-done | bytes 98336 | tf_op jit(solution)/shard_map/ppermute | solution.py:21
  54.2 25.8 %all_gather.3 = bf16[192,2048]{1,0:T(8,128)(2,1)S(1)} all-gather(bf16[24,2048]{1,0:T(8,128)(2,1)S(1)} %add_convert_fusion), channel_id=1, replica_groups=mesh['z'=8,'yh'=2,'c'=2,'feat'=4,'query'=4] {'z'}, dimensions={0}, use_global_device_ids=true | all-gather | bytes 884736 | tf_op jit(solution)/shard_map/all_gather | solution.py:59
  80.0 0.0 collective-permute-done.4
  80.0 1.4 convolution_convert_fusion.1
  81.4 1.4 convolution_convert_fusion
  82.7 0.0 copy-start.3
  82.8 0.0 copy-start.1
  82.8 0.0 copy-start.2
  82.8 0.9 pad_maximum_fusion
  83.7 6.7 %all-to-all-start.1 = ((bf16[4,48,1792]{2,1,0:T(8,128)(2,1)}), bf16[4,48,1792]{2,1,0:T(8,128)(2,1)S(1)}, u32[]{:S(2)}, u32[]{:S(2)}) async-start(bf16[4,48,1792]{2,1,0:T(8,128)(2,1)} %bitcast.3), calls=%async_computation.1 | async-start | bytes 1376256 | tf_op jit(solution)/shard_map/all_to_all | solution.py:70
  90.4 0.0 copy-done.3
  90.4 0.0 copy-done.1
  90.4 0.0 copy-done.2
  90.4 1.9 %collective-permute-start.2 = (s32[2,896]{1,0:T(2,128)S(1)}, s32[2,896]{1,0:T(2,128)S(1)}, u32[]{:S(2)}, u32[]{:S(2)}) collective-permute-start(s32[2,896]{1,0:T(2,128)S(1)} %pad_add_fusion.1), channel_id=1, source_target_pairs={{0,16},{16,0},{1,17},{17,1},{2,18},{18,2},{3,19},{19,3},{4,20},{20... | collective-permute-start | bytes 21512 | tf_op jit(solution)/shard_map/ppermute | solution.py:21
  92.4 0.3 fusion.3
  92.6 0.8 dynamic_slice.21
  93.4 0.1 collective-permute-done.2
  93.6 6.6 %all-to-all-done.1 = bf16[4,48,1792]{2,1,0:T(8,128)(2,1)S(1)} async-done(((bf16[4,48,1792]{2,1,0:T(8,128)(2,1)}), bf16[4,48,1792]{2,1,0:T(8,128)(2,1)S(1)}, u32[]{:S(2)}, u32[]{:S(2)}) %all-to-all-start.1) | async-done | bytes 688160 | tf_op jit(solution)/shard_map/all_to_all | solution.py:70
  100.1 0.1 convert_reduce_fusion.1
  100.2 0.6 fusion.15
  100.8 0.2 rev.3
  101.1 0.7 all_to_all.18
  101.8 8.8 %all-to-all-start.2 = ((f32[16,1,944]{2,1,0:T(1,128)}), f32[16,1,944]{2,1,0:T(1,128)S(1)}, u32[]{:S(2)}, u32[]{:S(2)}) async-start(f32[16,1,944]{2,1,0:T(1,128)} %all_to_all.18), calls=%async_computation.2 | async-start | bytes 131072 | tf_op jit(solution)/shard_map/all_to_all | solution.py:96
  110.6 6.7 %all-to-all-done.2 = f32[16,1,944]{2,1,0:T(1,128)S(1)} async-done(((f32[16,1,944]{2,1,0:T(1,128)}), f32[16,1,944]{2,1,0:T(1,128)S(1)}, u32[]{:S(2)}, u32[]{:S(2)}) %all-to-all-start.2) | async-done | bytes 60448 | tf_op jit(solution)/shard_map/all_to_all | solution.py:96
  117.4 0.1 reshape.42
  117.5 0.7 broadcast_in_dim.8
  118.2 5.6 %all-to-all-start.3 = ((f32[32,1,1280]{2,1,0:T(1,128)}), f32[32,1,1280]{2,1,0:T(1,128)S(1)}, u32[]{:S(2)}, u32[]{:S(2)}) async-start(f32[32,1,1280]{2,1,0:T(1,128)} %broadcast_in_dim.8), calls=%async_computation.3 | async-start | bytes 327680 | tf_op jit(solution)/shard_map/all_to_all | solution.py:25
  123.8 11.3 %all-to-all-done.3 = f32[32,1,1280]{2,1,0:T(1,128)S(1)} async-done(((f32[32,1,1280]{2,1,0:T(1,128)}), f32[32,1,1280]{2,1,0:T(1,128)S(1)}, u32[]{:S(2)}, u32[]{:S(2)}) %all-to-all-start.3) | async-done | bytes 163872 | tf_op jit(solution)/shard_map/all_to_all | solution.py:25
  135.1 0.4 reduce.2
  135.7 0.6 broadcast_multiply_fusion.1
  136.3 0.6 broadcast_multiply_fusion
  (26 shorter events, 0.4 us)
Async XLA Ops:
  0.6 2.1 %copy-start = (bf16[384,256]{1,0:T(8,128)(2,1)S(1)}, bf16[384,256]{1,0:T(8,128)(2,1)}, u32[]{:S(2)}) copy-start(bf16[384,256]{1,0:T(8,128)(2,1)} %param.7) | copy-start | bytes 589828
  0.6 6.3 %collective-permute-start.1 = (bf16[256,2048]{1,0:T(8,128)(2,1)}, bf16[256,2048]{1,0:T(8,128)(2,1)S(1)}, u32[]{:S(2)}, u32[]{:S(2)}) collective-permute-start(bf16[256,2048]{1,0:T(8,128)(2,1)} %param.8), channel_id=1, source_target_pairs={{0,16},{16,0},{1,17},{17,1},{2,18},{18,2},{3,19},{19,3},{4,20},{20... | collective-permute-start | bytes 3145736 | tf_op jit(solution)/shard_map/ppermute | solution.py:21
  2.7 4.2 %collective-permute-start = (bf16[192,256]{1,0:T(8,128)(2,1)S(1)}, bf16[192,256]{1,0:T(8,128)(2,1)S(1)}, u32[]{:S(2)}, u32[]{:S(2)}) collective-permute-start(bf16[192,256]{1,0:T(8,128)(2,1)S(1)} %constant_dynamic-slice_fusion.1), channel_id=1, source_target_pairs={{0,16},{16,0},{1,17},{17,1},{2,18},{18,2},{3,19},{19,3},{4,20},{20... | collective-permute-start | bytes 294920 | tf_op jit(solution)/shard_map/ppermute | solution.py:21
  5.2 2.4 %copy-start.4 = (bf16[896,2048]{1,0:T(8,128)(2,1)S(1)}, bf16[896,2048]{1,0:T(8,128)(2,1)}, u32[]{:S(2)}) copy-start(bf16[896,2048]{1,0:T(8,128)(2,1)} %param.9) | copy-start | bytes 11010052
  7.5 72.5 %collective-permute-start.4 = (bf16[896,2048]{1,0:T(8,128)(2,1)S(1)}, bf16[896,2048]{1,0:T(8,128)(2,1)S(1)}, u32[]{:S(2)}, u32[]{:S(2)}) collective-permute-start(bf16[896,2048]{1,0:T(8,128)(2,1)S(1)} %copy-done.4), channel_id=1, source_target_pairs={{0,16},{16,0},{1,17},{17,1},{2,18},{18,2},{3,19},{19,3},{4,20},{20... | collective-permute-start | bytes 11010056 | tf_op jit(solution)/shard_map/ppermute | solution.py:21
  43.5 10.6 %collective-permute-start.3 = (f16[24,2048]{1,0:T(8,128)(2,1)S(1)}, f16[24,2048]{1,0:T(8,128)(2,1)S(1)}, u32[]{:S(2)}, u32[]{:S(2)}) collective-permute-start(f16[24,2048]{1,0:T(8,128)(2,1)S(1)} %multiply_convert_fusion), channel_id=1, source_target_pairs={{0,32},{32,0},{1,33},{33,1},{2,34},{34,2},{3,35},{35,3},{4,36},{36... | collective-permute-start | bytes 294920 | tf_op jit(solution)/shard_map/ppermute | solution.py:21
  82.7 7.6 %copy-start.3 = (s32[256,2]{0,1:T(2,128)S(1)}, s32[256,2]{0,1:T(2,128)}, u32[]{:S(2)}) copy-start(s32[256,2]{0,1:T(2,128)} %param.12) | copy-start | bytes 6148
  82.8 7.6 %copy-start.1 = (s32[896]{0:T(1024)S(1)}, s32[896]{0:T(1024)}, u32[]{:S(2)}) copy-start(s32[896]{0:T(1024)} %param.13) | copy-start | bytes 10756
  82.8 7.6 %copy-start.2 = (s32[896]{0:T(1024)S(1)}, s32[896]{0:T(1024)}, u32[]{:S(2)}) copy-start(s32[896]{0:T(1024)} %param.11) | copy-start | bytes 10756
  83.7 16.5 %all-to-all-start.1 = ((bf16[4,48,1792]{2,1,0:T(8,128)(2,1)}), bf16[4,48,1792]{2,1,0:T(8,128)(2,1)S(1)}, u32[]{:S(2)}, u32[]{:S(2)}) async-start(bf16[4,48,1792]{2,1,0:T(8,128)(2,1)} %bitcast.3), calls=%async_computation.1 | async-start | bytes 1376256 | tf_op jit(solution)/shard_map/all_to_all | solution.py:70
  90.4 3.1 %collective-permute-start.2 = (s32[2,896]{1,0:T(2,128)S(1)}, s32[2,896]{1,0:T(2,128)S(1)}, u32[]{:S(2)}, u32[]{:S(2)}) collective-permute-start(s32[2,896]{1,0:T(2,128)S(1)} %pad_add_fusion.1), channel_id=1, source_target_pairs={{0,16},{16,0},{1,17},{17,1},{2,18},{18,2},{3,19},{19,3},{4,20},{20... | collective-permute-start | bytes 21512 | tf_op jit(solution)/shard_map/ppermute | solution.py:21
  101.8 15.5 %all-to-all-start.2 = ((f32[16,1,944]{2,1,0:T(1,128)}), f32[16,1,944]{2,1,0:T(1,128)S(1)}, u32[]{:S(2)}, u32[]{:S(2)}) async-start(f32[16,1,944]{2,1,0:T(1,128)} %all_to_all.18), calls=%async_computation.2 | async-start | bytes 131072 | tf_op jit(solution)/shard_map/all_to_all | solution.py:96
  118.2 16.9 %all-to-all-start.3 = ((f32[32,1,1280]{2,1,0:T(1,128)}), f32[32,1,1280]{2,1,0:T(1,128)S(1)}, u32[]{:S(2)}, u32[]{:S(2)}) async-start(f32[32,1,1280]{2,1,0:T(1,128)} %broadcast_in_dim.8), calls=%async_computation.3 | async-start | bytes 327680 | tf_op jit(solution)/shard_map/all_to_all | solution.py:25

commit v2 on v1

--- a/solution.py
+++ b/solution.py
@@ -88,23 +88,19 @@
     by_query = jnp.sum(bounded, axis=1)
     by_sample = jnp.sum(bounded, axis=0)
 
-    n_cf = CORES * n_f
     by_sample = by_sample.reshape(CORES, samples)
     by_sample = jnp.where(core == 0, by_sample, by_sample[::-1])
     both = jnp.concatenate([by_sample, jnp.broadcast_to(by_query[None], (CORES, rows))], axis=1)
-    both = jnp.broadcast_to(both[None, :, None], (Y_PARTS, CORES, n_f, samples + rows))
-    both = lax.all_to_all(both.reshape(Y_PARTS * n_cf, samples + rows), ("yh", "c", "feat"), 0, 0)
-    both = both.reshape(Y_PARTS, n_cf, samples + rows)
-    by_query = jnp.sum(both[:, :, samples:], axis=0).reshape(query_rows)
-    by_sample = lax.dynamic_index_in_dim(both, lax.axis_index("yh"), 0, False)[:, :samples]
-    by_sample = jnp.sum(by_sample, axis=0)
+    both = jnp.broadcast_to(both[None, :, None], (Y_PARTS, CORES, n_f * n_q, samples + rows))
+    both = both.reshape(Y_PARTS * CORES * n_f * n_q, samples + rows)
+    both = lax.all_to_all(both, ("yh", "c", "feat", "query"), 0, 0)
+    both = both.reshape(Y_PARTS, CORES * n_f, n_q, samples + rows)
+    by_query = lax.dynamic_index_in_dim(both, lax.axis_index("query"), 2, False)[:, :, samples:]
+    by_query = jnp.sum(by_query, axis=0).reshape(query_rows)
+    by_sample = lax.dynamic_index_in_dim(both, lax.axis_index("yh"), 0, False)[:, :, :samples]
+    by_sample = jnp.sum(by_sample, axis=(0, 1))
 
-    both = to_all(jnp.concatenate([by_sample, by_query]), ("z", "query"), n_z * n_q)
-    both = both.reshape(n_z, n_q, samples + query_rows)
-    by_sample = lax.dynamic_index_in_dim(both, lax.axis_index("z"), 0, False)[:, :samples]
-    by_query = lax.dynamic_index_in_dim(both, lax.axis_index("query"), 1, False)[:, samples:]
-    by_sample = jnp.sum(by_sample, axis=0)
-    by_query = jnp.sum(by_query, axis=0)
+    by_query = jnp.sum(to_all(by_query, "z", n_z), axis=0)
     all_queries = float(query_rows * n_q) ** (-0.5)
     all_samples = float(samples * n_t * CORES) ** (-0.5)
     return by_query * all_samples, by_sample * all_queries

time: 137 us -> 141 us (1.029)
  waiting for transfers between devices: 28.6 us -> 30.9 us
    all_to_all x1, waiting for transfers between devices: 6.74 us -> 13.4 us  [body(): both = lax.all_to_all(both, ('yh', 'c', 'feat', 'query'), 0, 0)]
    all_to_all x1, waiting for transfers between devices: 11.3 us -> 7.07 us  [to_all(): return lax.all_to_all(jnp.broadcast_to(x[None], (n,) + x.shape), axes, 0, 0)]
    all_to_all x1, starting transfers between devices: 8.76 us -> 11.8 us  [body(): both = lax.all_to_all(both, ('yh', 'c', 'feat', 'query'), 0, 0)]
    all_to_all x1, starting transfers between devices: 5.59 us -> 3.33 us  [to_all(): return lax.all_to_all(jnp.broadcast_to(x[None], (n,) + x.shape), axes, 0, 0)]
  transfers between devices with their start and end apart: 8 -> 8, of which waited for: 5 -> 5; matrix products, arithmetic and copies ran while one was open for 2% -> 3% of each run, Pallas kernels for 0% -> 0%
where the time goes in v2:
time: 141 us; the launch traced here: 140 us
  blocking collectives  59.7 us (42%)
  starting transfers between devices  36.9 us (26%)
  waiting for transfers between devices  30.9 us (22%)
  matrix products  5.71 us (4%)
  local copies, waits for them, and re-layouts  3.14 us (2%)
  other arithmetic  3.11 us (2%)
    all_to_all x1, blocking collectives, body(): pieces = lax.all_to_all(pieces, 'z', 0, 0)  33.9 us
    all_gather x1, blocking collectives, body(): whole = lax.all_gather(block.astype(BF16), 'z', axis=0, tiled=True)  25.8 us
    ppermute x5, starting transfers between devices, other(): return lax.ppermute(x, axis, [(i, i ^ step) for i in range(n)])  15.1 us
    all_to_all x1, waiting for transfers between devices, body(): both = lax.all_to_all(both, ('yh', 'c', 'feat', 'query'), 0, 0)  13.4 us
    all_to_all x1, starting transfers between devices, body(): both = lax.all_to_all(both, ('yh', 'c', 'feat', 'query'), 0, 0)  11.8 us
    all_to_all x1, waiting for transfers between devices, to_all(): return lax.all_to_all(jnp.broadcast_to(x[None], (n,) + x.shape), axes, 0, 0)  7.07 us
    all_to_all x1, starting transfers between devices, body(): score = lax.all_to_all(score.reshape(n_f, rows, 2 * samples), 'feat', 0, 0)  6.67 us
    all_to_all x1, waiting for transfers between devices, body(): score = lax.all_to_all(score.reshape(n_f, rows, 2 * samples), 'feat', 0, 0)  6.57 us
  transfers between devices with their start and end apart: 8, of which 5 were waited for; matrix products, arithmetic and copies ran while one was open for 3% of the time, Pallas kernels for 0%

profile of v2, /device:TPU:8, one launch (start us, length us, event | category | flops | bytes accessed | tf_op | source)
XLA Modules:
  0.0 140.5 jit_solution(2636445846627077791)
XLA Ops:
  0.6 0.0 copy-start
  0.6 2.1 %collective-permute-start.1 = (bf16[256,2048]{1,0:T(8,128)(2,1)}, bf16[256,2048]{1,0:T(8,128)(2,1)S(1)}, u32[]{:S(2)}, u32[]{:S(2)}) collective-permute-start(bf16[256,2048]{1,0:T(8,128)(2,1)} %param.8), channel_id=1, source_target_pairs={{0,16},{16,0},{1,17},{17,1},{2,18},{18,2},{3,19},{19,3},{4,20},{20... | collective-permute-start | bytes 3145736 | tf_op jit(solution)/shard_map/ppermute | solution.py:21
  2.7 0.0 copy-done
  2.7 2.4 %collective-permute-start = (bf16[192,256]{1,0:T(8,128)(2,1)S(1)}, bf16[192,256]{1,0:T(8,128)(2,1)S(1)}, u32[]{:S(2)}, u32[]{:S(2)}) collective-permute-start(bf16[192,256]{1,0:T(8,128)(2,1)S(1)} %constant_dynamic-slice_fusion.1), channel_id=1, source_target_pairs={{0,16},{16,0},{1,17},{17,1},{2,18},{18,2},{3,19},{19,3},{4,20},{20... | collective-permute-start | bytes 294920 | tf_op jit(solution)/shard_map/ppermute | solution.py:21
  5.2 0.0 copy-start.4
  5.2 1.8 %fusion.5 = f32[192,2048]{1,0:T(8,128)S(1)} fusion(bf16[256,2048]{1,0:T(8,128)(2,1)} %param.8, bf16[384,256]{1,0:T(8,128)(2,1)S(1)} %copy-done, s32[]{:T(128)S(6)} %select_n.27), kind=kOutput, calls=%fused_computation.21 | convolution fusion | flops 201326592 | bytes 2719748 | tf_op jit(solution)/shard_map/dot_general | solution.py:44
  6.9 0.0 collective-permute-done
  6.9 0.0 collective-permute-done.1
  7.0 0.4 fusion.1
  7.3 0.2 copy-done.4
  7.5 1.9 %collective-permute-start.4 = (bf16[896,2048]{1,0:T(8,128)(2,1)S(1)}, bf16[896,2048]{1,0:T(8,128)(2,1)S(1)}, u32[]{:S(2)}, u32[]{:S(2)}) collective-permute-start(bf16[896,2048]{1,0:T(8,128)(2,1)S(1)} %copy-done.4), channel_id=1, source_target_pairs={{0,16},{16,0},{1,17},{17,1},{2,18},{18,2},{3,19},{19,3},{4,20},{20... | collective-permute-start | bytes 11010056 | tf_op jit(solution)/shard_map/ppermute | solution.py:21
  9.4 33.9 %all_to_all.25 = f16[8,24,2048]{2,1,0:T(8,128)(2,1)S(1)} all-to-all(f16[8,24,2048]{2,1,0:T(8,128)(2,1)S(1)} %bitcast.19), channel_id=1, replica_groups=mesh['z'=8,'yh'=2,'c'=2,'feat'=4,'query'=4] {'z'}, dimensions={0} | all-to-all | bytes 1572864 | tf_op jit(solution)/shard_map/all_to_all | solution.py:55
  43.3 0.1 convert_reduce_fusion
  43.5 6.8 %collective-permute-start.3 = (f16[24,2048]{1,0:T(8,128)(2,1)S(1)}, f16[24,2048]{1,0:T(8,128)(2,1)S(1)}, u32[]{:S(2)}, u32[]{:S(2)}) collective-permute-start(f16[24,2048]{1,0:T(8,128)(2,1)S(1)} %multiply_convert_fusion), channel_id=1, source_target_pairs={{0,32},{32,0},{1,33},{33,1},{2,34},{34,2},{3,35},{35,3},{4,36},{36... | collective-permute-start | bytes 294920 | tf_op jit(solution)/shard_map/ppermute | solution.py:21
  50.3 3.8 %collective-permute-done.3 = f16[24,2048]{1,0:T(8,128)(2,1)S(1)} collective-permute-done((f16[24,2048]{1,0:T(8,128)(2,1)S(1)}, f16[24,2048]{1,0:T(8,128)(2,1)S(1)}, u32[]{:S(2)}, u32[]{:S(2)}) %collective-permute-start.3) | collective-permute-done | bytes 98336 | tf_op jit(solution)/shard_map/ppermute | solution.py:21
  54.2 25.8 %all_gather.3 = bf16[192,2048]{1,0:T(8,128)(2,1)S(1)} all-gather(bf16[24,2048]{1,0:T(8,128)(2,1)S(1)} %add_convert_fusion), channel_id=1, replica_groups=mesh['z'=8,'yh'=2,'c'=2,'feat'=4,'query'=4] {'z'}, dimensions={0}, use_global_device_ids=true | all-gather | bytes 884736 | tf_op jit(solution)/shard_map/all_gather | solution.py:59
  80.0 0.0 collective-permute-done.4
  80.0 1.4 convolution_convert_fusion.1
  81.4 1.4 convolution_convert_fusion
  82.7 0.0 copy-start.3
  82.8 0.0 copy-start.1
  82.8 0.0 copy-start.2
  82.8 0.9 pad_maximum_fusion
  83.7 6.7 %all-to-all-start.1 = ((bf16[4,48,1792]{2,1,0:T(8,128)(2,1)}), bf16[4,48,1792]{2,1,0:T(8,128)(2,1)S(1)}, u32[]{:S(2)}, u32[]{:S(2)}) async-start(bf16[4,48,1792]{2,1,0:T(8,128)(2,1)} %bitcast.3), calls=%async_computation.1 | async-start | bytes 1376256 | tf_op jit(solution)/shard_map/all_to_all | solution.py:70
  90.4 0.0 copy-done.3
  90.4 0.0 copy-done.1
  90.4 0.0 copy-done.2
  90.4 1.9 %collective-permute-start.2 = (s32[2,896]{1,0:T(2,128)S(1)}, s32[2,896]{1,0:T(2,128)S(1)}, u32[]{:S(2)}, u32[]{:S(2)}) collective-permute-start(s32[2,896]{1,0:T(2,128)S(1)} %pad_add_fusion.1), channel_id=1, source_target_pairs={{0,16},{16,0},{1,17},{17,1},{2,18},{18,2},{3,19},{19,3},{4,20},{20... | collective-permute-start | bytes 21512 | tf_op jit(solution)/shard_map/ppermute | solution.py:21
  92.4 0.3 fusion.3
  92.6 0.8 dynamic_slice.17
  93.4 0.1 collective-permute-done.2
  93.6 6.6 %all-to-all-done.1 = bf16[4,48,1792]{2,1,0:T(8,128)(2,1)S(1)} async-done(((bf16[4,48,1792]{2,1,0:T(8,128)(2,1)}), bf16[4,48,1792]{2,1,0:T(8,128)(2,1)S(1)}, u32[]{:S(2)}, u32[]{:S(2)}) %all-to-all-start.1) | async-done | bytes 688160 | tf_op jit(solution)/shard_map/all_to_all | solution.py:70
  100.1 0.1 convert_reduce_fusion.1
  100.2 0.6 fusion.15
  100.8 0.2 rev.3
  101.1 1.0 all_to_all.18
  102.1 11.8 %all-to-all-start.2 = ((f32[64,1,944]{2,1,0:T(1,128)}), f32[64,1,944]{2,1,0:T(1,128)S(1)}, u32[]{:S(2)}, u32[]{:S(2)}) async-start(f32[64,1,944]{2,1,0:T(1,128)} %all_to_all.18), calls=%async_computation.2 | async-start | bytes 524288 | tf_op jit(solution)/shard_map/all_to_all | solution.py:96
  113.9 13.4 %all-to-all-done.2 = f32[64,1,944]{2,1,0:T(1,128)S(1)} async-done(((f32[64,1,944]{2,1,0:T(1,128)}), f32[64,1,944]{2,1,0:T(1,128)S(1)}, u32[]{:S(2)}, u32[]{:S(2)}) %all-to-all-start.2) | async-done | bytes 241696 | tf_op jit(solution)/shard_map/all_to_all | solution.py:96
  127.3 0.6 reduce.3
  127.9 0.1 reshape.36
  128.0 0.1 constant_dynamic-slice_fusion
  128.1 0.1 broadcast_in_dim.10
  128.2 0.6 broadcast_in_dim.11
  128.8 3.3 %all-to-all-start.3 = ((f32[8,1,384]{2,1,0:T(1,128)}), f32[8,1,384]{2,1,0:T(1,128)S(1)}, u32[]{:S(2)}, u32[]{:S(2)}) async-start(f32[8,1,384]{2,1,0:T(1,128)} %broadcast_in_dim.11), calls=%async_computation.3 | async-start | bytes 24576 | tf_op jit(solution)/shard_map/all_to_all | solution.py:25
  132.2 0.6 broadcast_multiply_fusion
  132.8 7.1 %all-to-all-done.3 = f32[8,1,384]{2,1,0:T(1,128)S(1)} async-done(((f32[8,1,384]{2,1,0:T(1,128)}), f32[8,1,384]{2,1,0:T(1,128)S(1)}, u32[]{:S(2)}, u32[]{:S(2)}) %all-to-all-start.3) | async-done | bytes 12320 | tf_op jit(solution)/shard_map/all_to_all | solution.py:25
  139.9 0.6 broadcast_multiply_fusion.1
  (20 shorter events, 0.3 us)
Async XLA Ops:
  0.6 2.1 %copy-start = (bf16[384,256]{1,0:T(8,128)(2,1)S(1)}, bf16[384,256]{1,0:T(8,128)(2,1)}, u32[]{:S(2)}) copy-start(bf16[384,256]{1,0:T(8,128)(2,1)} %param.7) | copy-start | bytes 589828
  0.6 6.3 %collective-permute-start.1 = (bf16[256,2048]{1,0:T(8,128)(2,1)}, bf16[256,2048]{1,0:T(8,128)(2,1)S(1)}, u32[]{:S(2)}, u32[]{:S(2)}) collective-permute-start(bf16[256,2048]{1,0:T(8,128)(2,1)} %param.8), channel_id=1, source_target_pairs={{0,16},{16,0},{1,17},{17,1},{2,18},{18,2},{3,19},{19,3},{4,20},{20... | collective-permute-start | bytes 3145736 | tf_op jit(solution)/shard_map/ppermute | solution.py:21
  2.7 4.2 %collective-permute-start = (bf16[192,256]{1,0:T(8,128)(2,1)S(1)}, bf16[192,256]{1,0:T(8,128)(2,1)S(1)}, u32[]{:S(2)}, u32[]{:S(2)}) collective-permute-start(bf16[192,256]{1,0:T(8,128)(2,1)S(1)} %constant_dynamic-slice_fusion.1), channel_id=1, source_target_pairs={{0,16},{16,0},{1,17},{17,1},{2,18},{18,2},{3,19},{19,3},{4,20},{20... | collective-permute-start | bytes 294920 | tf_op jit(solution)/shard_map/ppermute | solution.py:21
  5.2 2.4 %copy-start.4 = (bf16[896,2048]{1,0:T(8,128)(2,1)S(1)}, bf16[896,2048]{1,0:T(8,128)(2,1)}, u32[]{:S(2)}) copy-start(bf16[896,2048]{1,0:T(8,128)(2,1)} %param.9) | copy-start | bytes 11010052
  7.5 72.5 %collective-permute-start.4 = (bf16[896,2048]{1,0:T(8,128)(2,1)S(1)}, bf16[896,2048]{1,0:T(8,128)(2,1)S(1)}, u32[]{:S(2)}, u32[]{:S(2)}) collective-permute-start(bf16[896,2048]{1,0:T(8,128)(2,1)S(1)} %copy-done.4), channel_id=1, source_target_pairs={{0,16},{16,0},{1,17},{17,1},{2,18},{18,2},{3,19},{19,3},{4,20},{20... | collective-permute-start | bytes 11010056 | tf_op jit(solution)/shard_map/ppermute | solution.py:21
  43.5 10.6 %collective-permute-start.3 = (f16[24,2048]{1,0:T(8,128)(2,1)S(1)}, f16[24,2048]{1,0:T(8,128)(2,1)S(1)}, u32[]{:S(2)}, u32[]{:S(2)}) collective-permute-start(f16[24,2048]{1,0:T(8,128)(2,1)S(1)} %multiply_convert_fusion), channel_id=1, source_target_pairs={{0,32},{32,0},{1,33},{33,1},{2,34},{34,2},{3,35},{35,3},{4,36},{36... | collective-permute-start | bytes 294920 | tf_op jit(solution)/shard_map/ppermute | solution.py:21
  82.7 7.6 %copy-start.3 = (s32[256,2]{0,1:T(2,128)S(1)}, s32[256,2]{0,1:T(2,128)}, u32[]{:S(2)}) copy-start(s32[256,2]{0,1:T(2,128)} %param.12) | copy-start | bytes 6148
  82.8 7.6 %copy-start.1 = (s32[896]{0:T(1024)S(1)}, s32[896]{0:T(1024)}, u32[]{:S(2)}) copy-start(s32[896]{0:T(1024)} %param.13) | copy-start | bytes 10756
  82.8 7.6 %copy-start.2 = (s32[896]{0:T(1024)S(1)}, s32[896]{0:T(1024)}, u32[]{:S(2)}) copy-start(s32[896]{0:T(1024)} %param.11) | copy-start | bytes 10756
  83.7 16.5 %all-to-all-start.1 = ((bf16[4,48,1792]{2,1,0:T(8,128)(2,1)}), bf16[4,48,1792]{2,1,0:T(8,128)(2,1)S(1)}, u32[]{:S(2)}, u32[]{:S(2)}) async-start(bf16[4,48,1792]{2,1,0:T(8,128)(2,1)} %bitcast.3), calls=%async_computation.1 | async-start | bytes 1376256 | tf_op jit(solution)/shard_map/all_to_all | solution.py:70
  90.4 3.1 %collective-permute-start.2 = (s32[2,896]{1,0:T(2,128)S(1)}, s32[2,896]{1,0:T(2,128)S(1)}, u32[]{:S(2)}, u32[]{:S(2)}) collective-permute-start(s32[2,896]{1,0:T(2,128)S(1)} %pad_add_fusion.1), channel_id=1, source_target_pairs={{0,16},{16,0},{1,17},{17,1},{2,18},{18,2},{3,19},{19,3},{4,20},{20... | collective-permute-start | bytes 21512 | tf_op jit(solution)/shard_map/ppermute | solution.py:21
  102.1 25.1 %all-to-all-start.2 = ((f32[64,1,944]{2,1,0:T(1,128)}), f32[64,1,944]{2,1,0:T(1,128)S(1)}, u32[]{:S(2)}, u32[]{:S(2)}) async-start(f32[64,1,944]{2,1,0:T(1,128)} %all_to_all.18), calls=%async_computation.2 | async-start | bytes 524288 | tf_op jit(solution)/shard_map/all_to_all | solution.py:96
  128.8 11.1 %all-to-all-start.3 = ((f32[8,1,384]{2,1,0:T(1,128)}), f32[8,1,384]{2,1,0:T(1,128)S(1)}, u32[]{:S(2)}, u32[]{:S(2)}) async-start(f32[8,1,384]{2,1,0:T(1,128)} %broadcast_in_dim.11), calls=%async_computation.3 | async-start | bytes 24576 | tf_op jit(solution)/shard_map/all_to_all | solution.py:25

commit v3 on v1

--- a/solution.py
+++ b/solution.py
@@ -29,7 +29,7 @@
     n_z, n_f, n_q = lax.axis_size("z"), lax.axis_size("feat"), lax.axis_size("query")
     n_t = n_z * Y_PARTS
     core = lax.axis_index("c")
-    lane = lax.axis_index("feat")
+    lane = jnp.where(core == 0, lax.axis_index("feat"), n_f - 1 - lax.axis_index("feat"))
     query_rows, depth = queries.shape
     width = precond.shape[1]
     samples = train_feats.shape[0]
@@ -52,11 +52,12 @@
     feats_other = other(train_feats, "c")
     ids = jnp.stack([train_shard, log_weight])
     ids = jnp.concatenate([ids, other(ids, "c")], axis=1)
-    pieces = lax.all_to_all(pieces, "z", 0, 0)
+    lines = [[CORES * i for i in range(n_z)], [CORES * i + 1 for i in reversed(range(n_z))]]
+    pieces = lax.all_to_all(pieces, ("z", "c"), 0, 0, axis_index_groups=lines)
     block = jnp.sum(pieces.astype(F32), axis=0)
     sent = (block * (1.0 / n_z)).astype(F16)
     block = block * (1.0 / up) + other(sent, "yh").astype(F32) * (n_z / up)
-    whole = lax.all_gather(block.astype(BF16), "z", axis=0, tiled=True)
+    whole = lax.all_gather(block.astype(BF16), ("z", "c"), axis=0, tiled=True, axis_index_groups=lines)
     whole, feats_other = lax.optimization_barrier((whole, feats_other))
 
     dims = (((1,), (1,)), ((), ()))
@@ -67,7 +68,8 @@
         ],
         axis=1,
     )
-    score = lax.all_to_all(score.reshape(n_f, rows, 2 * samples), "feat", 0, 0)
+    lanes = [list(range(n_f)), [n_f + i for i in reversed(range(n_f))]]
+    score = lax.all_to_all(score.reshape(n_f, rows, 2 * samples), ("c", "feat"), 0, 0, axis_index_groups=lanes)
     score = jnp.sum(score.astype(F32), axis=0) * float(feat) ** (-0.5)
 
     active = jnp.minimum(
@@ -95,7 +97,8 @@
     both = jnp.broadcast_to(both[None, :, None], (Y_PARTS, CORES, n_f, samples + rows))
     both = lax.all_to_all(both.reshape(Y_PARTS * n_cf, samples + rows), ("yh", "c", "feat"), 0, 0)
     both = both.reshape(Y_PARTS, n_cf, samples + rows)
-    by_query = jnp.sum(both[:, :, samples:], axis=0).reshape(query_rows)
+    by_query = jnp.sum(both[:, :, samples:], axis=0).reshape(CORES, n_f, rows)
+    by_query = jnp.concatenate([by_query[0], by_query[1, ::-1]]).reshape(query_rows)
     by_sample = lax.dynamic_index_in_dim(both, lax.axis_index("yh"), 0, False)[:, :samples]
     by_sample = jnp.sum(by_sample, axis=0)
 

time: 137 us -> 137 us (level)
  blocking collectives: 59.7 us -> 58.1 us
    all_to_all x1, blocking collectives: 33.9 us -> 31.1 us  [body(): pieces = lax.all_to_all(pieces, ('z', 'c'), 0, 0, axis_index_groups=lines)]
where the time goes in v3:
time: 137 us; the launch traced here: 136 us
  blocking collectives  58.1 us (42%)
  starting transfers between devices  36.6 us (27%)
  waiting for transfers between devices  29.1 us (21%)
  matrix products  5.71 us (4%)
  local copies, waits for them, and re-layouts  2.92 us (2%)
  other arithmetic  2.88 us (2%)
    all_to_all x1, blocking collectives, body(): pieces = lax.all_to_all(pieces, ('z', 'c'), 0, 0, axis_index_groups=lines)  31.1 us
    all_gather x1, blocking collectives, body(): lax.all_gather(block.astype(BF16), ('z', 'c'), axis=0, tiled=True, axis_i...  27.1 us
    ppermute x5, starting transfers between devices, other(): return lax.ppermute(x, axis, [(i, i ^ step) for i in range(n)])  15.1 us
    all_to_all x1, waiting for transfers between devices, to_all(): return lax.all_to_all(jnp.broadcast_to(x[None], (n,) + x.shape), axes, 0, 0)  11.3 us
    all_to_all x1, starting transfers between devices, body(): lax.all_to_all(both.reshape(Y_PARTS * n_cf, samples + rows), ('yh', 'c',...  8.92 us
    all_to_all x1, waiting for transfers between devices, body(): lax.all_to_all(both.reshape(Y_PARTS * n_cf, samples + rows), ('yh', 'c',...  6.74 us
    all_to_all x1, starting transfers between devices, to_all(): return lax.all_to_all(jnp.broadcast_to(x[None], (n,) + x.shape), axes, 0, 0)  6.63 us
    all_to_all x1, waiting for transfers between devices, body(): lax.all_to_all(score.reshape(n_f, rows, 2 * samples), ('c', 'feat'), 0, 0...  6.57 us
  transfers between devices with their start and end apart: 8, of which 5 were waited for; matrix products, arithmetic and copies ran while one was open for 2% of the time, Pallas kernels for 0%

profile of v3, /device:TPU:8, one launch (start us, length us, event | category | flops | bytes accessed | tf_op | source)
XLA Modules:
  0.0 136.4 jit_solution(3130169212538255325)
XLA Ops:
  0.6 0.0 copy-start
  0.6 2.1 %collective-permute-start.1 = (bf16[256,2048]{1,0:T(8,128)(2,1)}, bf16[256,2048]{1,0:T(8,128)(2,1)S(1)}, u32[]{:S(2)}, u32[]{:S(2)}) collective-permute-start(bf16[256,2048]{1,0:T(8,128)(2,1)} %param.8), channel_id=1, source_target_pairs={{0,16},{16,0},{1,17},{17,1},{2,18},{18,2},{3,19},{19,3},{4,20},{20... | collective-permute-start | bytes 3145736 | tf_op jit(solution)/shard_map/ppermute | solution.py:21
  2.7 0.0 copy-done
  2.7 2.4 %collective-permute-start = (bf16[192,256]{1,0:T(8,128)(2,1)S(1)}, bf16[192,256]{1,0:T(8,128)(2,1)S(1)}, u32[]{:S(2)}, u32[]{:S(2)}) collective-permute-start(bf16[192,256]{1,0:T(8,128)(2,1)S(1)} %constant_dynamic-slice_fusion.1), channel_id=1, source_target_pairs={{0,16},{16,0},{1,17},{17,1},{2,18},{18,2},{3,19},{19,3},{4,20},{20... | collective-permute-start | bytes 294920 | tf_op jit(solution)/shard_map/ppermute | solution.py:21
  5.2 0.0 copy-start.4
  5.2 1.8 %fusion.5 = f32[192,2048]{1,0:T(8,128)S(1)} fusion(bf16[256,2048]{1,0:T(8,128)(2,1)} %param.8, bf16[384,256]{1,0:T(8,128)(2,1)S(1)} %copy-done, s32[]{:T(128)S(6)} %select_n.36), kind=kOutput, calls=%fused_computation.19 | convolution fusion | flops 201326592 | bytes 2719748 | tf_op jit(solution)/shard_map/dot_general | solution.py:44
  6.9 0.0 collective-permute-done
  6.9 0.0 collective-permute-done.1
  7.0 0.4 fusion.1
  7.3 0.2 copy-done.4
  7.5 1.9 %collective-permute-start.4 = (bf16[896,2048]{1,0:T(8,128)(2,1)S(1)}, bf16[896,2048]{1,0:T(8,128)(2,1)S(1)}, u32[]{:S(2)}, u32[]{:S(2)}) collective-permute-start(bf16[896,2048]{1,0:T(8,128)(2,1)S(1)} %copy-done.4), channel_id=1, source_target_pairs={{0,16},{16,0},{1,17},{17,1},{2,18},{18,2},{3,19},{19,3},{4,20},{20... | collective-permute-start | bytes 11010056 | tf_op jit(solution)/shard_map/ppermute | solution.py:21
  9.4 31.1 %all_to_all.25 = f16[8,24,2048]{2,1,0:T(8,128)(2,1)S(1)} all-to-all(f16[8,24,2048]{2,1,0:T(8,128)(2,1)S(1)} %bitcast.22), channel_id=1, replica_groups={{0,64,128,192,256,320,384,448},{464,400,336,272,208,144,80,16},{1,65,12..., dimensions={0} | all-to-all | bytes 1572864 | tf_op jit(solution)/shard_map/all_to_all | solution.py:56
  40.5 0.1 convert_reduce_fusion
  40.6 6.8 %collective-permute-start.3 = (f16[24,2048]{1,0:T(8,128)(2,1)S(1)}, f16[24,2048]{1,0:T(8,128)(2,1)S(1)}, u32[]{:S(2)}, u32[]{:S(2)}) collective-permute-start(f16[24,2048]{1,0:T(8,128)(2,1)S(1)} %multiply_convert_fusion), channel_id=1, source_target_pairs={{0,32},{32,0},{1,33},{33,1},{2,34},{34,2},{3,35},{35,3},{4,36},{36... | collective-permute-start | bytes 294920 | tf_op jit(solution)/shard_map/ppermute | solution.py:21
  47.5 4.4 %collective-permute-done.3 = f16[24,2048]{1,0:T(8,128)(2,1)S(1)} collective-permute-done((f16[24,2048]{1,0:T(8,128)(2,1)S(1)}, f16[24,2048]{1,0:T(8,128)(2,1)S(1)}, u32[]{:S(2)}, u32[]{:S(2)}) %collective-permute-start.3) | collective-permute-done | bytes 98336 | tf_op jit(solution)/shard_map/ppermute | solution.py:21
  51.9 27.1 %all_gather.3 = bf16[192,2048]{1,0:T(8,128)(2,1)S(1)} all-gather(bf16[24,2048]{1,0:T(8,128)(2,1)S(1)} %add_convert_fusion), channel_id=1, replica_groups={{0,64,128,192,256,320,384,448},{464,400,336,272,208,144,80,16},{1,65,12..., dimensions={0}, use_global_device_ids=true | all-gather | bytes 884736 | tf_op jit(solution)/shard_map/all_gather | solution.py:60
  79.0 0.0 collective-permute-done.4
  79.0 1.4 convolution_convert_fusion.1
  80.4 1.4 convolution_convert_fusion
  81.7 0.0 copy-start.3
  81.7 0.0 copy-start.1
  81.8 0.0 copy-start.2
  81.8 0.9 pad_maximum_fusion
  82.7 6.0 %all-to-all-start.1 = ((bf16[4,48,1792]{2,1,0:T(8,128)(2,1)}), bf16[4,48,1792]{2,1,0:T(8,128)(2,1)S(1)}, u32[]{:S(2)}, u32[]{:S(2)}) async-start(bf16[4,48,1792]{2,1,0:T(8,128)(2,1)} %bitcast.3), calls=%async_computation.1 | async-start | bytes 1376256 | tf_op jit(solution)/shard_map/all_to_all | solution.py:72
  88.6 0.0 copy-done.3
  88.6 0.0 copy-done.1
  88.7 0.0 copy-done.2
  88.7 1.9 %collective-permute-start.2 = (s32[2,896]{1,0:T(2,128)S(1)}, s32[2,896]{1,0:T(2,128)S(1)}, u32[]{:S(2)}, u32[]{:S(2)}) collective-permute-start(s32[2,896]{1,0:T(2,128)S(1)} %pad_add_fusion.1), channel_id=1, source_target_pairs={{0,16},{16,0},{1,17},{17,1},{2,18},{18,2},{3,19},{19,3},{4,20},{20... | collective-permute-start | bytes 21512 | tf_op jit(solution)/shard_map/ppermute | solution.py:21
  90.6 0.3 fusion.3
  90.9 0.8 dynamic_slice.21
  91.7 0.1 collective-permute-done.2
  91.9 6.6 %all-to-all-done.1 = bf16[4,48,1792]{2,1,0:T(8,128)(2,1)S(1)} async-done(((bf16[4,48,1792]{2,1,0:T(8,128)(2,1)}), bf16[4,48,1792]{2,1,0:T(8,128)(2,1)S(1)}, u32[]{:S(2)}, u32[]{:S(2)}) %all-to-all-start.1) | async-done | bytes 688160 | tf_op jit(solution)/shard_map/all_to_all | solution.py:72
  98.4 0.1 convert_reduce_fusion.1
  98.5 0.6 fusion.15
  99.1 0.2 rev.4
  99.4 0.7 all_to_all.18
  100.1 8.9 %all-to-all-start.2 = ((f32[16,1,944]{2,1,0:T(1,128)}), f32[16,1,944]{2,1,0:T(1,128)S(1)}, u32[]{:S(2)}, u32[]{:S(2)}) async-start(f32[16,1,944]{2,1,0:T(1,128)} %all_to_all.18), calls=%async_computation.2 | async-start | bytes 131072 | tf_op jit(solution)/shard_map/all_to_all | solution.py:98
  109.0 6.7 %all-to-all-done.2 = f32[16,1,944]{2,1,0:T(1,128)S(1)} async-done(((f32[16,1,944]{2,1,0:T(1,128)}), f32[16,1,944]{2,1,0:T(1,128)S(1)}, u32[]{:S(2)}, u32[]{:S(2)}) %all-to-all-start.2) | async-done | bytes 60448 | tf_op jit(solution)/shard_map/all_to_all | solution.py:98
  115.8 0.1 reshape.48
  116.0 0.7 broadcast_in_dim.8
  116.7 6.6 %all-to-all-start.3 = ((f32[32,1,1280]{2,1,0:T(1,128)}), f32[32,1,1280]{2,1,0:T(1,128)S(1)}, u32[]{:S(2)}, u32[]{:S(2)}) async-start(f32[32,1,1280]{2,1,0:T(1,128)} %broadcast_in_dim.8), calls=%async_computation.3 | async-start | bytes 327680 | tf_op jit(solution)/shard_map/all_to_all | solution.py:25
  123.3 11.3 %all-to-all-done.3 = f32[32,1,1280]{2,1,0:T(1,128)S(1)} async-done(((f32[32,1,1280]{2,1,0:T(1,128)}), f32[32,1,1280]{2,1,0:T(1,128)S(1)}, u32[]{:S(2)}, u32[]{:S(2)}) %all-to-all-start.3) | async-done | bytes 163872 | tf_op jit(solution)/shard_map/all_to_all | solution.py:25
  134.7 0.4 reduce.2
  135.2 0.6 broadcast_multiply_fusion.1
  135.8 0.6 broadcast_multiply_fusion
  (29 shorter events, 0.4 us)
Async XLA Ops:
  0.6 2.1 %copy-start = (bf16[384,256]{1,0:T(8,128)(2,1)S(1)}, bf16[384,256]{1,0:T(8,128)(2,1)}, u32[]{:S(2)}) copy-start(bf16[384,256]{1,0:T(8,128)(2,1)} %param.7) | copy-start | bytes 589828
  0.6 6.3 %collective-permute-start.1 = (bf16[256,2048]{1,0:T(8,128)(2,1)}, bf16[256,2048]{1,0:T(8,128)(2,1)S(1)}, u32[]{:S(2)}, u32[]{:S(2)}) collective-permute-start(bf16[256,2048]{1,0:T(8,128)(2,1)} %param.8), channel_id=1, source_target_pairs={{0,16},{16,0},{1,17},{17,1},{2,18},{18,2},{3,19},{19,3},{4,20},{20... | collective-permute-start | bytes 3145736 | tf_op jit(solution)/shard_map/ppermute | solution.py:21
  2.7 4.2 %collective-permute-start = (bf16[192,256]{1,0:T(8,128)(2,1)S(1)}, bf16[192,256]{1,0:T(8,128)(2,1)S(1)}, u32[]{:S(2)}, u32[]{:S(2)}) collective-permute-start(bf16[192,256]{1,0:T(8,128)(2,1)S(1)} %constant_dynamic-slice_fusion.1), channel_id=1, source_target_pairs={{0,16},{16,0},{1,17},{17,1},{2,18},{18,2},{3,19},{19,3},{4,20},{20... | collective-permute-start | bytes 294920 | tf_op jit(solution)/shard_map/ppermute | solution.py:21
  5.2 2.4 %copy-start.4 = (bf16[896,2048]{1,0:T(8,128)(2,1)S(1)}, bf16[896,2048]{1,0:T(8,128)(2,1)}, u32[]{:S(2)}) copy-start(bf16[896,2048]{1,0:T(8,128)(2,1)} %param.9) | copy-start | bytes 11010052
  7.5 71.5 %collective-permute-start.4 = (bf16[896,2048]{1,0:T(8,128)(2,1)S(1)}, bf16[896,2048]{1,0:T(8,128)(2,1)S(1)}, u32[]{:S(2)}, u32[]{:S(2)}) collective-permute-start(bf16[896,2048]{1,0:T(8,128)(2,1)S(1)} %copy-done.4), channel_id=1, source_target_pairs={{0,16},{16,0},{1,17},{17,1},{2,18},{18,2},{3,19},{19,3},{4,20},{20... | collective-permute-start | bytes 11010056 | tf_op jit(solution)/shard_map/ppermute | solution.py:21
  40.6 11.2 %collective-permute-start.3 = (f16[24,2048]{1,0:T(8,128)(2,1)S(1)}, f16[24,2048]{1,0:T(8,128)(2,1)S(1)}, u32[]{:S(2)}, u32[]{:S(2)}) collective-permute-start(f16[24,2048]{1,0:T(8,128)(2,1)S(1)} %multiply_convert_fusion), channel_id=1, source_target_pairs={{0,32},{32,0},{1,33},{33,1},{2,34},{34,2},{3,35},{35,3},{4,36},{36... | collective-permute-start | bytes 294920 | tf_op jit(solution)/shard_map/ppermute | solution.py:21
  81.7 6.9 %copy-start.3 = (s32[256,2]{0,1:T(2,128)S(1)}, s32[256,2]{0,1:T(2,128)}, u32[]{:S(2)}) copy-start(s32[256,2]{0,1:T(2,128)} %param.12) | copy-start | bytes 6148
  81.7 6.9 %copy-start.1 = (s32[896]{0:T(1024)S(1)}, s32[896]{0:T(1024)}, u32[]{:S(2)}) copy-start(s32[896]{0:T(1024)} %param.13) | copy-start | bytes 10756
  81.8 6.9 %copy-start.2 = (s32[896]{0:T(1024)S(1)}, s32[896]{0:T(1024)}, u32[]{:S(2)}) copy-start(s32[896]{0:T(1024)} %param.11) | copy-start | bytes 10756
  82.7 15.8 %all-to-all-start.1 = ((bf16[4,48,1792]{2,1,0:T(8,128)(2,1)}), bf16[4,48,1792]{2,1,0:T(8,128)(2,1)S(1)}, u32[]{:S(2)}, u32[]{:S(2)}) async-start(bf16[4,48,1792]{2,1,0:T(8,128)(2,1)} %bitcast.3), calls=%async_computation.1 | async-start | bytes 1376256 | tf_op jit(solution)/shard_map/all_to_all | solution.py:72
  88.7 3.1 %collective-permute-start.2 = (s32[2,896]{1,0:T(2,128)S(1)}, s32[2,896]{1,0:T(2,128)S(1)}, u32[]{:S(2)}, u32[]{:S(2)}) collective-permute-start(s32[2,896]{1,0:T(2,128)S(1)} %pad_add_fusion.1), channel_id=1, source_target_pairs={{0,16},{16,0},{1,17},{17,1},{2,18},{18,2},{3,19},{19,3},{4,20},{20... | collective-permute-start | bytes 21512 | tf_op jit(solution)/shard_map/ppermute | solution.py:21
  100.1 15.7 %all-to-all-start.2 = ((f32[16,1,944]{2,1,0:T(1,128)}), f32[16,1,944]{2,1,0:T(1,128)S(1)}, u32[]{:S(2)}, u32[]{:S(2)}) async-start(f32[16,1,944]{2,1,0:T(1,128)} %all_to_all.18), calls=%async_computation.2 | async-start | bytes 131072 | tf_op jit(solution)/shard_map/all_to_all | solution.py:98
  116.7 18.0 %all-to-all-start.3 = ((f32[32,1,1280]{2,1,0:T(1,128)}), f32[32,1,1280]{2,1,0:T(1,128)S(1)}, u32[]{:S(2)}, u32[]{:S(2)}) async-start(f32[32,1,1280]{2,1,0:T(1,128)} %broadcast_in_dim.8), calls=%async_computation.3 | async-start | bytes 327680 | tf_op jit(solution)/shard_map/all_to_all | solution.py:25

commit v4 on v2

--- a/solution.py
+++ b/solution.py
@@ -29,7 +29,7 @@
     n_z, n_f, n_q = lax.axis_size("z"), lax.axis_size("feat"), lax.axis_size("query")
     n_t = n_z * Y_PARTS
     core = lax.axis_index("c")
-    lane = lax.axis_index("feat")
+    lane = jnp.where(core == 0, lax.axis_index("feat"), n_f - 1 - lax.axis_index("feat"))
     query_rows, depth = queries.shape
     width = precond.shape[1]
     samples = train_feats.shape[0]
@@ -52,11 +52,12 @@
     feats_other = other(train_feats, "c")
     ids = jnp.stack([train_shard, log_weight])
     ids = jnp.concatenate([ids, other(ids, "c")], axis=1)
-    pieces = lax.all_to_all(pieces, "z", 0, 0)
+    lines = [[CORES * i for i in range(n_z)], [CORES * i + 1 for i in reversed(range(n_z))]]
+    pieces = lax.all_to_all(pieces, ("z", "c"), 0, 0, axis_index_groups=lines)
     block = jnp.sum(pieces.astype(F32), axis=0)
     sent = (block * (1.0 / n_z)).astype(F16)
     block = block * (1.0 / up) + other(sent, "yh").astype(F32) * (n_z / up)
-    whole = lax.all_gather(block.astype(BF16), "z", axis=0, tiled=True)
+    whole = lax.all_gather(block.astype(BF16), ("z", "c"), axis=0, tiled=True, axis_index_groups=lines)
     whole, feats_other = lax.optimization_barrier((whole, feats_other))
 
     dims = (((1,), (1,)), ((), ()))
@@ -67,7 +68,8 @@
         ],
         axis=1,
     )
-    score = lax.all_to_all(score.reshape(n_f, rows, 2 * samples), "feat", 0, 0)
+    lanes = [list(range(n_f)), [n_f + i for i in reversed(range(n_f))]]
+    score = lax.all_to_all(score.reshape(n_f, rows, 2 * samples), ("c", "feat"), 0, 0, axis_index_groups=lanes)
     score = jnp.sum(score.astype(F32), axis=0) * float(feat) ** (-0.5)
 
     active = jnp.minimum(
@@ -88,15 +90,16 @@
     by_query = jnp.sum(bounded, axis=1)
     by_sample = jnp.sum(bounded, axis=0)
 
-    by_sample = by_sample.reshape(CORES, samples)
-    by_sample = jnp.where(core == 0, by_sample, by_sample[::-1])
-    both = jnp.concatenate([by_sample, jnp.broadcast_to(by_query[None], (CORES, rows))], axis=1)
-    both = jnp.broadcast_to(both[None, :, None], (Y_PARTS, CORES, n_f * n_q, samples + rows))
-    both = both.reshape(Y_PARTS * CORES * n_f * n_q, samples + rows)
-    both = lax.all_to_all(both, ("yh", "c", "feat", "query"), 0, 0)
-    both = both.reshape(Y_PARTS, CORES * n_f, n_q, samples + rows)
+    both = jnp.concatenate([by_sample[samples:], by_query])
+    both = other(both, "c")
+    by_sample = by_sample[:samples] + both[:samples]
+    by_query, theirs = jnp.where(core == 0, by_query, both[samples:]), jnp.where(core == 0, both[samples:], by_query)
+
+    both = to_all(jnp.concatenate([by_sample, by_query, theirs]), ("yh", "feat", "query"), Y_PARTS * n_f * n_q)
+    both = both.reshape(Y_PARTS, n_f, n_q, samples + CORES * rows)
     by_query = lax.dynamic_index_in_dim(both, lax.axis_index("query"), 2, False)[:, :, samples:]
-    by_query = jnp.sum(by_query, axis=0).reshape(query_rows)
+    by_query = jnp.sum(by_query, axis=0)
+    by_query = jnp.concatenate([by_query[:, :rows], by_query[::-1, rows:]]).reshape(query_rows)
     by_sample = lax.dynamic_index_in_dim(both, lax.axis_index("yh"), 0, False)[:, :, :samples]
     by_sample = jnp.sum(by_sample, axis=(0, 1))
 

time: 141 us -> 138 us (0.979)
  waiting for transfers between devices: 30.9 us -> 29.2 us
  blocking collectives: 59.7 us -> 58.1 us
    all_to_all x2 -> x1, waiting for transfers between devices: 19.9 us -> 6.57 us  [body(): lax.all_to_all(score.reshape(n_f, rows, 2 * samples), ('c', 'feat'), 0, 0...]
    all_to_all x2 -> x1, starting transfers between devices: 18.4 us -> 5.97 us  [body(): lax.all_to_all(score.reshape(n_f, rows, 2 * samples), ('c', 'feat'), 0, 0...]
    all_to_all x1 -> x2, starting transfers between devices: 3.33 us -> 15.3 us  [to_all(): return lax.all_to_all(jnp.broadcast_to(x[None], (n,) + x.shape), axes, 0, 0)]
    all_to_all x1 -> x2, waiting for transfers between devices: 7.07 us -> 17 us  [to_all(): return lax.all_to_all(jnp.broadcast_to(x[None], (n,) + x.shape), axes, 0, 0)]
    all_to_all x1, blocking collectives: 33.9 us -> 31.1 us  [body(): pieces = lax.all_to_all(pieces, ('z', 'c'), 0, 0, axis_index_groups=lines)]
    ppermute x5 -> x6, starting transfers between devices: 15.1 us -> 17 us  [other(): return lax.ppermute(x, axis, [(i, i ^ step) for i in range(n)])]
    ppermute x5 -> x6, waiting for transfers between devices: 3.92 us -> 5.62 us  [other(): return lax.ppermute(x, axis, [(i, i ^ step) for i in range(n)])]
  transfers between devices with their start and end apart: 8 -> 9, of which waited for: 5 -> 6; matrix products, arithmetic and copies ran while one was open for 3% -> 3% of each run, Pallas kernels for 0% -> 0%
where the time goes in v4:
time: 138 us
  blocking collectives  58.1 us (42%)
  starting transfers between devices  38.3 us (28%)
  waiting for transfers between devices  29.2 us (21%)
  matrix products  5.71 us (4%)
  other arithmetic  2.88 us (2%)
  local copies, waits for them, and re-layouts  2.61 us (2%)
    all_to_all x1, blocking collectives, body(): pieces = lax.all_to_all(pieces, ('z', 'c'), 0, 0, axis_index_groups=lines)  31.1 us
    all_gather x1, blocking collectives, body(): lax.all_gather(block.astype(BF16), ('z', 'c'), axis=0, tiled=True, axis_i...  27.1 us
    ppermute x6, starting transfers between devices, other(): return lax.ppermute(x, axis, [(i, i ^ step) for i in range(n)])  17 us
    all_to_all x2, waiting for transfers between devices, to_all(): return lax.all_to_all(jnp.broadcast_to(x[None], (n,) + x.shape), axes, 0, 0)  17 us
    all_to_all x2, starting transfers between devices, to_all(): return lax.all_to_all(jnp.broadcast_to(x[None], (n,) + x.shape), axes, 0, 0)  15.3 us
    all_to_all x1, waiting for transfers between devices, body(): lax.all_to_all(score.reshape(n_f, rows, 2 * samples), ('c', 'feat'), 0, 0...  6.57 us
    all_to_all x1, starting transfers between devices, body(): lax.all_to_all(score.reshape(n_f, rows, 2 * samples), ('c', 'feat'), 0, 0...  5.97 us
    ppermute x6, waiting for transfers between devices, other(): return lax.ppermute(x, axis, [(i, i ^ step) for i in range(n)])  5.62 us
  transfers between devices with their start and end apart: 9, of which 6 were waited for; matrix products, arithmetic and copies ran while one was open for 3% of the time, Pallas kernels for 0%

profile of v4, /device:TPU:8, one launch (start us, length us, event | category | flops | bytes accessed | tf_op | source)
XLA Modules:
  0.0 137.8 jit_solution(9422064914110651481)
XLA Ops:
  0.6 0.0 copy-start
  0.6 2.1 %collective-permute-start.1 = (bf16[256,2048]{1,0:T(8,128)(2,1)}, bf16[256,2048]{1,0:T(8,128)(2,1)S(1)}, u32[]{:S(2)}, u32[]{:S(2)}) collective-permute-start(bf16[256,2048]{1,0:T(8,128)(2,1)} %param.8), channel_id=1, source_target_pairs={{0,16},{16,0},{1,17},{17,1},{2,18},{18,2},{3,19},{19,3},{4,20},{20... | collective-permute-start | bytes 3145736 | tf_op jit(solution)/shard_map/ppermute | solution.py:21
  2.7 0.0 copy-done
  2.7 2.4 %collective-permute-start = (bf16[192,256]{1,0:T(8,128)(2,1)S(1)}, bf16[192,256]{1,0:T(8,128)(2,1)S(1)}, u32[]{:S(2)}, u32[]{:S(2)}) collective-permute-start(bf16[192,256]{1,0:T(8,128)(2,1)S(1)} %constant_dynamic-slice_fusion.1), channel_id=1, source_target_pairs={{0,16},{16,0},{1,17},{17,1},{2,18},{18,2},{3,19},{19,3},{4,20},{20... | collective-permute-start | bytes 294920 | tf_op jit(solution)/shard_map/ppermute | solution.py:21
  5.2 0.0 copy-start.4
  5.2 1.8 %fusion.5 = f32[192,2048]{1,0:T(8,128)S(1)} fusion(bf16[256,2048]{1,0:T(8,128)(2,1)} %param.8, bf16[384,256]{1,0:T(8,128)(2,1)S(1)} %copy-done, s32[]{:T(128)S(6)} %select_n.35), kind=kOutput, calls=%fused_computation.19 | convolution fusion | flops 201326592 | bytes 2719748 | tf_op jit(solution)/shard_map/dot_general | solution.py:44
  6.9 0.0 collective-permute-done
  6.9 0.0 collective-permute-done.1
  7.0 0.4 fusion.1
  7.3 0.2 copy-done.4
  7.5 1.9 %collective-permute-start.4 = (bf16[896,2048]{1,0:T(8,128)(2,1)S(1)}, bf16[896,2048]{1,0:T(8,128)(2,1)S(1)}, u32[]{:S(2)}, u32[]{:S(2)}) collective-permute-start(bf16[896,2048]{1,0:T(8,128)(2,1)S(1)} %copy-done.4), channel_id=1, source_target_pairs={{0,16},{16,0},{1,17},{17,1},{2,18},{18,2},{3,19},{19,3},{4,20},{20... | collective-permute-start | bytes 11010056 | tf_op jit(solution)/shard_map/ppermute | solution.py:21
  9.4 31.1 %all_to_all.22 = f16[8,24,2048]{2,1,0:T(8,128)(2,1)S(1)} all-to-all(f16[8,24,2048]{2,1,0:T(8,128)(2,1)S(1)} %bitcast.17), channel_id=1, replica_groups={{0,64,128,192,256,320,384,448},{464,400,336,272,208,144,80,16},{1,65,12..., dimensions={0} | all-to-all | bytes 1572864 | tf_op jit(solution)/shard_map/all_to_all | solution.py:56
  40.5 0.1 convert_reduce_fusion
  40.6 6.8 %collective-permute-start.3 = (f16[24,2048]{1,0:T(8,128)(2,1)S(1)}, f16[24,2048]{1,0:T(8,128)(2,1)S(1)}, u32[]{:S(2)}, u32[]{:S(2)}) collective-permute-start(f16[24,2048]{1,0:T(8,128)(2,1)S(1)} %multiply_convert_fusion), channel_id=1, source_target_pairs={{0,32},{32,0},{1,33},{33,1},{2,34},{34,2},{3,35},{35,3},{4,36},{36... | collective-permute-start | bytes 294920 | tf_op jit(solution)/shard_map/ppermute | solution.py:21
  47.5 4.4 %collective-permute-done.3 = f16[24,2048]{1,0:T(8,128)(2,1)S(1)} collective-permute-done((f16[24,2048]{1,0:T(8,128)(2,1)S(1)}, f16[24,2048]{1,0:T(8,128)(2,1)S(1)}, u32[]{:S(2)}, u32[]{:S(2)}) %collective-permute-start.3) | collective-permute-done | bytes 98336 | tf_op jit(solution)/shard_map/ppermute | solution.py:21
  51.9 27.1 %all_gather.3 = bf16[192,2048]{1,0:T(8,128)(2,1)S(1)} all-gather(bf16[24,2048]{1,0:T(8,128)(2,1)S(1)} %add_convert_fusion), channel_id=1, replica_groups={{0,64,128,192,256,320,384,448},{464,400,336,272,208,144,80,16},{1,65,12..., dimensions={0}, use_global_device_ids=true | all-gather | bytes 884736 | tf_op jit(solution)/shard_map/all_gather | solution.py:60
  79.0 0.0 collective-permute-done.4
  79.0 1.4 convolution_convert_fusion.1
  80.4 1.4 convolution_convert_fusion
  81.7 0.0 copy-start.3
  81.7 0.0 copy-start.1
  81.8 0.0 copy-start.2
  81.8 0.9 pad_maximum_fusion
  82.7 6.0 %all-to-all-start.1 = ((bf16[4,48,1792]{2,1,0:T(8,128)(2,1)}), bf16[4,48,1792]{2,1,0:T(8,128)(2,1)S(1)}, u32[]{:S(2)}, u32[]{:S(2)}) async-start(bf16[4,48,1792]{2,1,0:T(8,128)(2,1)} %bitcast.3), calls=%async_computation.1 | async-start | bytes 1376256 | tf_op jit(solution)/shard_map/all_to_all | solution.py:72
  88.6 0.0 copy-done.3
  88.6 0.0 copy-done.1
  88.7 0.0 copy-done.2
  88.7 1.9 %collective-permute-start.2 = (s32[2,896]{1,0:T(2,128)S(1)}, s32[2,896]{1,0:T(2,128)S(1)}, u32[]{:S(2)}, u32[]{:S(2)}) collective-permute-start(s32[2,896]{1,0:T(2,128)S(1)} %pad_add_fusion.1), channel_id=1, source_target_pairs={{0,16},{16,0},{1,17},{17,1},{2,18},{18,2},{3,19},{19,3},{4,20},{20... | collective-permute-start | bytes 21512 | tf_op jit(solution)/shard_map/ppermute | solution.py:21
  90.6 0.3 fusion.3
  90.9 0.8 dynamic_slice.17
  91.7 0.1 collective-permute-done.2
  91.9 6.6 %all-to-all-done.1 = bf16[4,48,1792]{2,1,0:T(8,128)(2,1)S(1)} async-done(((bf16[4,48,1792]{2,1,0:T(8,128)(2,1)}), bf16[4,48,1792]{2,1,0:T(8,128)(2,1)S(1)}, u32[]{:S(2)}, u32[]{:S(2)}) %all-to-all-start.1) | async-done | bytes 688160 | tf_op jit(solution)/shard_map/all_to_all | solution.py:72
  98.4 0.1 convert_reduce_fusion.1
  98.5 0.6 fusion.15
  99.1 1.9 %collective-permute-start.5 = (f32[944]{0:T(1024)S(1)}, f32[944]{0:T(1024)S(1)}, u32[]{:S(2)}, u32[]{:S(2)}) collective-permute-start(f32[944]{0:T(1024)S(1)} %pad_maximum_fusion.1), channel_id=1, source_target_pairs={{0,16},{16,0},{1,17},{17,1},{2,18},{18,2},{3,19},{19,3},{4,20},{20... | collective-permute-start | bytes 11336 | tf_op jit(solution)/shard_map/ppermute | solution.py:21
  101.1 1.1 collective-permute-done.5
  102.2 0.1 pad_maximum_fusion.2
  102.3 0.7 broadcast_in_dim.6
  103.0 11.5 %all-to-all-start.2 = ((f32[32,1,992]{2,1,0:T(1,128)}), f32[32,1,992]{2,1,0:T(1,128)S(1)}, u32[]{:S(2)}, u32[]{:S(2)}) async-start(f32[32,1,992]{2,1,0:T(1,128)} %broadcast_in_dim.6), calls=%async_computation.2 | async-start | bytes 262144 | tf_op jit(solution)/shard_map/all_to_all | solution.py:25
  114.5 9.9 %all-to-all-done.2 = f32[32,1,992]{2,1,0:T(1,128)S(1)} async-done(((f32[32,1,992]{2,1,0:T(1,128)}), f32[32,1,992]{2,1,0:T(1,128)S(1)}, u32[]{:S(2)}, u32[]{:S(2)}) %all-to-all-start.2) | async-done | bytes 127008 | tf_op jit(solution)/shard_map/all_to_all | solution.py:25
  124.4 0.3 reduce.3
  124.9 0.1 fusion.16
  125.0 0.1 broadcast_in_dim.7
  125.1 0.6 broadcast_in_dim.8
  125.7 3.8 %all-to-all-start.3 = ((f32[8,1,384]{2,1,0:T(1,128)}), f32[8,1,384]{2,1,0:T(1,128)S(1)}, u32[]{:S(2)}, u32[]{:S(2)}) async-start(f32[8,1,384]{2,1,0:T(1,128)} %broadcast_in_dim.8), calls=%async_computation.3 | async-start | bytes 24576 | tf_op jit(solution)/shard_map/all_to_all | solution.py:25
  129.5 0.6 broadcast_multiply_fusion
  130.1 7.1 %all-to-all-done.3 = f32[8,1,384]{2,1,0:T(1,128)S(1)} async-done(((f32[8,1,384]{2,1,0:T(1,128)}), f32[8,1,384]{2,1,0:T(1,128)S(1)}, u32[]{:S(2)}, u32[]{:S(2)}) %all-to-all-start.3) | async-done | bytes 12320 | tf_op jit(solution)/shard_map/all_to_all | solution.py:25
  137.2 0.6 broadcast_multiply_fusion.1
  (23 shorter events, 0.4 us)
Async XLA Ops:
  0.6 2.1 %copy-start = (bf16[384,256]{1,0:T(8,128)(2,1)S(1)}, bf16[384,256]{1,0:T(8,128)(2,1)}, u32[]{:S(2)}) copy-start(bf16[384,256]{1,0:T(8,128)(2,1)} %param.7) | copy-start | bytes 589828
  0.6 6.3 %collective-permute-start.1 = (bf16[256,2048]{1,0:T(8,128)(2,1)}, bf16[256,2048]{1,0:T(8,128)(2,1)S(1)}, u32[]{:S(2)}, u32[]{:S(2)}) collective-permute-start(bf16[256,2048]{1,0:T(8,128)(2,1)} %param.8), channel_id=1, source_target_pairs={{0,16},{16,0},{1,17},{17,1},{2,18},{18,2},{3,19},{19,3},{4,20},{20... | collective-permute-start | bytes 3145736 | tf_op jit(solution)/shard_map/ppermute | solution.py:21
  2.7 4.2 %collective-permute-start = (bf16[192,256]{1,0:T(8,128)(2,1)S(1)}, bf16[192,256]{1,0:T(8,128)(2,1)S(1)}, u32[]{:S(2)}, u32[]{:S(2)}) collective-permute-start(bf16[192,256]{1,0:T(8,128)(2,1)S(1)} %constant_dynamic-slice_fusion.1), channel_id=1, source_target_pairs={{0,16},{16,0},{1,17},{17,1},{2,18},{18,2},{3,19},{19,3},{4,20},{20... | collective-permute-start | bytes 294920 | tf_op jit(solution)/shard_map/ppermute | solution.py:21
  5.2 2.4 %copy-start.4 = (bf16[896,2048]{1,0:T(8,128)(2,1)S(1)}, bf16[896,2048]{1,0:T(8,128)(2,1)}, u32[]{:S(2)}) copy-start(bf16[896,2048]{1,0:T(8,128)(2,1)} %param.9) | copy-start | bytes 11010052
  7.5 71.5 %collective-permute-start.4 = (bf16[896,2048]{1,0:T(8,128)(2,1)S(1)}, bf16[896,2048]{1,0:T(8,128)(2,1)S(1)}, u32[]{:S(2)}, u32[]{:S(2)}) collective-permute-start(bf16[896,2048]{1,0:T(8,128)(2,1)S(1)} %copy-done.4), channel_id=1, source_target_pairs={{0,16},{16,0},{1,17},{17,1},{2,18},{18,2},{3,19},{19,3},{4,20},{20... | collective-permute-start | bytes 11010056 | tf_op jit(solution)/shard_map/ppermute | solution.py:21
  40.6 11.2 %collective-permute-start.3 = (f16[24,2048]{1,0:T(8,128)(2,1)S(1)}, f16[24,2048]{1,0:T(8,128)(2,1)S(1)}, u32[]{:S(2)}, u32[]{:S(2)}) collective-permute-start(f16[24,2048]{1,0:T(8,128)(2,1)S(1)} %multiply_convert_fusion), channel_id=1, source_target_pairs={{0,32},{32,0},{1,33},{33,1},{2,34},{34,2},{3,35},{35,3},{4,36},{36... | collective-permute-start | bytes 294920 | tf_op jit(solution)/shard_map/ppermute | solution.py:21
  81.7 6.9 %copy-start.3 = (s32[256,2]{0,1:T(2,128)S(1)}, s32[256,2]{0,1:T(2,128)}, u32[]{:S(2)}) copy-start(s32[256,2]{0,1:T(2,128)} %param.12) | copy-start | bytes 6148
  81.7 6.9 %copy-start.1 = (s32[896]{0:T(1024)S(1)}, s32[896]{0:T(1024)}, u32[]{:S(2)}) copy-start(s32[896]{0:T(1024)} %param.13) | copy-start | bytes 10756
  81.8 6.9 %copy-start.2 = (s32[896]{0:T(1024)S(1)}, s32[896]{0:T(1024)}, u32[]{:S(2)}) copy-start(s32[896]{0:T(1024)} %param.11) | copy-start | bytes 10756
  82.7 15.8 %all-to-all-start.1 = ((bf16[4,48,1792]{2,1,0:T(8,128)(2,1)}), bf16[4,48,1792]{2,1,0:T(8,128)(2,1)S(1)}, u32[]{:S(2)}, u32[]{:S(2)}) async-start(bf16[4,48,1792]{2,1,0:T(8,128)(2,1)} %bitcast.3), calls=%async_computation.1 | async-start | bytes 1376256 | tf_op jit(solution)/shard_map/all_to_all | solution.py:72
  88.7 3.1 %collective-permute-start.2 = (s32[2,896]{1,0:T(2,128)S(1)}, s32[2,896]{1,0:T(2,128)S(1)}, u32[]{:S(2)}, u32[]{:S(2)}) collective-permute-start(s32[2,896]{1,0:T(2,128)S(1)} %pad_add_fusion.1), channel_id=1, source_target_pairs={{0,16},{16,0},{1,17},{17,1},{2,18},{18,2},{3,19},{19,3},{4,20},{20... | collective-permute-start | bytes 21512 | tf_op jit(solution)/shard_map/ppermute | solution.py:21
  99.1 3.1 %collective-permute-start.5 = (f32[944]{0:T(1024)S(1)}, f32[944]{0:T(1024)S(1)}, u32[]{:S(2)}, u32[]{:S(2)}) collective-permute-start(f32[944]{0:T(1024)S(1)} %pad_maximum_fusion.1), channel_id=1, source_target_pairs={{0,16},{16,0},{1,17},{17,1},{2,18},{18,2},{3,19},{19,3},{4,20},{20... | collective-permute-start | bytes 11336 | tf_op jit(solution)/shard_map/ppermute | solution.py:21
  103.0 21.4 %all-to-all-start.2 = ((f32[32,1,992]{2,1,0:T(1,128)}), f32[32,1,992]{2,1,0:T(1,128)S(1)}, u32[]{:S(2)}, u32[]{:S(2)}) async-start(f32[32,1,992]{2,1,0:T(1,128)} %broadcast_in_dim.6), calls=%async_computation.2 | async-start | bytes 262144 | tf_op jit(solution)/shard_map/all_to_all | solution.py:25
  125.7 11.5 %all-to-all-start.3 = ((f32[8,1,384]{2,1,0:T(1,128)}), f32[8,1,384]{2,1,0:T(1,128)S(1)}, u32[]{:S(2)}, u32[]{:S(2)}) async-start(f32[8,1,384]{2,1,0:T(1,128)} %broadcast_in_dim.8), calls=%async_computation.3 | async-start | bytes 24576 | tf_op jit(solution)/shard_map/all_to_all | solution.py:25

commit v5 on v3

--- a/solution.py
+++ b/solution.py
@@ -39,19 +39,17 @@
 
     mine = lax.dynamic_slice_in_dim(queries, core * half, half, 0)
     yours = lax.dynamic_slice_in_dim(queries, (1 - core) * half, half, 0)
-    precond_other = other(precond, "c")
-    theirs = other(yours, "c")
-    part = jnp.dot(mine, precond, preferred_element_type=F32) + jnp.dot(
-        theirs, precond_other, preferred_element_type=F32
+    up = 128.0
+    sent = (jnp.dot(yours, precond, preferred_element_type=F32) * (CORES * up)).astype(F16)
+    sent, mine, train_feats, train_shard, log_weight = lax.optimization_barrier(
+        (sent, mine, train_feats, train_shard, log_weight)
     )
-    up = 128.0
-    pieces = (part * up).astype(F16).reshape(n_z, half // n_z, width)
-    pieces, train_feats, train_shard, log_weight = lax.optimization_barrier(
-        (pieces, train_feats, train_shard, log_weight)
-    )
+    theirs = other(sent, "c")
     feats_other = other(train_feats, "c")
     ids = jnp.stack([train_shard, log_weight])
     ids = jnp.concatenate([ids, other(ids, "c")], axis=1)
+    part = jnp.dot(mine, precond, preferred_element_type=F32) + theirs.astype(F32) * (1.0 / (CORES * up))
+    pieces = (part * up).astype(F16).reshape(n_z, half // n_z, width)
     lines = [[CORES * i for i in range(n_z)], [CORES * i + 1 for i in reversed(range(n_z))]]
     pieces = lax.all_to_all(pieces, ("z", "c"), 0, 0, axis_index_groups=lines)
     block = jnp.sum(pieces.astype(F32), axis=0)

time: 137 us -> 136 us (level)
  starting transfers between devices: 36.6 us -> 34.9 us
    ppermute x5 -> x4, starting transfers between devices: 15.1 us -> 13.1 us  [other(): return lax.ppermute(x, axis, [(i, i ^ step) for i in range(n)])]
    ppermute x5 -> x4, waiting for transfers between devices: 4.49 us -> 3.83 us  [other(): return lax.ppermute(x, axis, [(i, i ^ step) for i in range(n)])]
  transfers between devices with their start and end apart: 8 -> 7, of which waited for: 5 -> 5; matrix products, arithmetic and copies ran while one was open for 2% -> 1% of each run, Pallas kernels for 0% -> 0%
where the time goes in v5:
time: 136 us; the launch traced here: 135 us
  blocking collectives  58.7 us (43%)
  starting transfers between devices  34.9 us (26%)
  waiting for transfers between devices  28.5 us (21%)
  matrix products  5.31 us (4%)
  local copies, waits for them, and re-layouts  3.99 us (3%)
  other arithmetic  2.88 us (2%)
    all_to_all x1, blocking collectives, body(): pieces = lax.all_to_all(pieces, ('z', 'c'), 0, 0, axis_index_groups=lines)  30.9 us
    all_gather x1, blocking collectives, body(): lax.all_gather(block.astype(BF16), ('z', 'c'), axis=0, tiled=True, axis_i...  27.8 us
    ppermute x4, starting transfers between devices, other(): return lax.ppermute(x, axis, [(i, i ^ step) for i in range(n)])  13.1 us
    all_to_all x1, waiting for transfers between devices, to_all(): return lax.all_to_all(jnp.broadcast_to(x[None], (n,) + x.shape), axes, 0, 0)  11.3 us
    all_to_all x1, starting transfers between devices, body(): lax.all_to_all(both.reshape(Y_PARTS * n_cf, samples + rows), ('yh', 'c',...  8.83 us
    all_to_all x1, starting transfers between devices, to_all(): return lax.all_to_all(jnp.broadcast_to(x[None], (n,) + x.shape), axes, 0, 0)  6.75 us
    all_to_all x1, waiting for transfers between devices, body(): lax.all_to_all(both.reshape(Y_PARTS * n_cf, samples + rows), ('yh', 'c',...  6.74 us
    all_to_all x1, waiting for transfers between devices, body(): lax.all_to_all(score.reshape(n_f, rows, 2 * samples), ('c', 'feat'), 0, 0...  6.59 us
  transfers between devices with their start and end apart: 7, of which 5 were waited for; matrix products, arithmetic and copies ran while one was open for 1% of the time, Pallas kernels for 0%

profile of v5, /device:TPU:8, one launch (start us, length us, event | category | flops | bytes accessed | tf_op | source)
XLA Modules:
  0.0 135.2 jit_solution(8182885374602126383)
XLA Ops:
  0.6 0.0 copy-start
  0.7 1.0 constant_dynamic-slice_fusion.1
  1.6 0.3 copy-done
  1.9 1.3 fusion
  3.2 1.9 %collective-permute-start.1 = (f16[192,2048]{1,0:T(8,128)(2,1)S(1)}, f16[192,2048]{1,0:T(8,128)(2,1)S(1)}, u32[]{:S(2)}, u32[]{:S(2)}) collective-permute-start(f16[192,2048]{1,0:T(8,128)(2,1)S(1)} %fusion), channel_id=1, source_target_pairs={{0,16},{16,0},{1,17},{17,1},{2,18},{18,2},{3,19},{19,3},{4,20},{20... | collective-permute-start | bytes 2359304 | tf_op jit(solution)/shard_map/ppermute | solution.py:21
  5.1 2.4 %collective-permute-start.3 = (bf16[896,2048]{1,0:T(8,128)(2,1)}, bf16[896,2048]{1,0:T(8,128)(2,1)S(1)}, u32[]{:S(2)}, u32[]{:S(2)}) collective-permute-start(bf16[896,2048]{1,0:T(8,128)(2,1)} %param.9), channel_id=1, source_target_pairs={{0,16},{16,0},{1,17},{17,1},{2,18},{18,2},{3,19},{19,3},{4,20},{20... | collective-permute-start | bytes 11010056 | tf_op jit(solution)/shard_map/ppermute | solution.py:21
  7.5 0.0 collective-permute-done.1
  7.5 0.5 multiply_convert_fusion
  8.0 0.0 copy-start.4
  8.0 30.9 %all_to_all.25 = f16[8,24,2048]{2,1,0:T(8,128)(2,1)S(1)} all-to-all(f16[8,24,2048]{2,1,0:T(8,128)(2,1)S(1)} %bitcast.22), channel_id=1, replica_groups={{0,64,128,192,256,320,384,448},{464,400,336,272,208,144,80,16},{1,65,12..., dimensions={0} | all-to-all | bytes 1572864 | tf_op jit(solution)/shard_map/all_to_all | solution.py:54
  38.9 0.1 convert_reduce_fusion
  39.1 6.8 %collective-permute-start.2 = (f16[24,2048]{1,0:T(8,128)(2,1)S(1)}, f16[24,2048]{1,0:T(8,128)(2,1)S(1)}, u32[]{:S(2)}, u32[]{:S(2)}) collective-permute-start(f16[24,2048]{1,0:T(8,128)(2,1)S(1)} %multiply_convert_fusion.1), channel_id=1, source_target_pairs={{0,32},{32,0},{1,33},{33,1},{2,34},{34,2},{3,35},{35,3},{4,36},{36... | collective-permute-start | bytes 294920 | tf_op jit(solution)/shard_map/ppermute | solution.py:21
  45.9 3.7 %collective-permute-done.2 = f16[24,2048]{1,0:T(8,128)(2,1)S(1)} collective-permute-done((f16[24,2048]{1,0:T(8,128)(2,1)S(1)}, f16[24,2048]{1,0:T(8,128)(2,1)S(1)}, u32[]{:S(2)}, u32[]{:S(2)}) %collective-permute-start.2) | collective-permute-done | bytes 98336 | tf_op jit(solution)/shard_map/ppermute | solution.py:21
  49.7 27.8 %all_gather.3 = bf16[192,2048]{1,0:T(8,128)(2,1)S(1)} all-gather(bf16[24,2048]{1,0:T(8,128)(2,1)S(1)} %add_convert_fusion), channel_id=1, replica_groups={{0,64,128,192,256,320,384,448},{464,400,336,272,208,144,80,16},{1,65,12..., dimensions={0}, use_global_device_ids=true | all-gather | bytes 884736 | tf_op jit(solution)/shard_map/all_gather | solution.py:58
  77.5 0.0 collective-permute-done.3
  77.5 0.0 copy-done.4
  77.5 1.4 %convolution_convert_fusion.1 = bf16[192,896]{1,0:T(8,128)(2,1)S(1)} fusion(bf16[192,2048]{1,0:T(8,128)(2,1)S(1)} %all_gather.3, bf16[896,2048]{1,0:T(8,128)(2,1)S(1)} %copy-done.4), kind=kOutput, calls=%fused_computation.8 | convolution fusion | flops 704815104 | bytes 4800512 | tf_op jit(solution)/shard_map/dot_general | solution.py:64
  78.9 1.4 %convolution_convert_fusion = bf16[192,896]{1,0:T(8,128)(2,1)S(1)} fusion(bf16[192,2048]{1,0:T(8,128)(2,1)S(1)} %all_gather.3, bf16[896,2048]{1,0:T(8,128)(2,1)S(1)} %collective-permute-done.3), kind=kOutput, calls=%fused_computation.7 | convolution fusion | flops 704815104 | bytes 4800512 | tf_op jit(solution)/shard_map/dot_general | solution.py:65
  80.2 0.0 copy-start.1
  80.2 0.0 copy-start.2
  80.3 0.0 copy-start.3
  80.3 0.9 pad_maximum_fusion
  81.2 6.2 %all-to-all-start.1 = ((bf16[4,48,1792]{2,1,0:T(8,128)(2,1)}), bf16[4,48,1792]{2,1,0:T(8,128)(2,1)S(1)}, u32[]{:S(2)}, u32[]{:S(2)}) async-start(bf16[4,48,1792]{2,1,0:T(8,128)(2,1)} %bitcast.3), calls=%async_computation.1 | async-start | bytes 1376256 | tf_op jit(solution)/shard_map/all_to_all | solution.py:70
  87.4 0.0 copy-done.1
  87.4 0.0 copy-done.2
  87.5 1.9 %collective-permute-start = (s32[2,896]{1,0:T(2,128)S(1)}, s32[2,896]{1,0:T(2,128)S(1)}, u32[]{:S(2)}, u32[]{:S(2)}) collective-permute-start(s32[2,896]{1,0:T(2,128)S(1)} %pad_add_fusion.1), channel_id=1, source_target_pairs={{0,16},{16,0},{1,17},{17,1},{2,18},{18,2},{3,19},{19,3},{4,20},{20... | collective-permute-start | bytes 21512 | tf_op jit(solution)/shard_map/ppermute | solution.py:21
  89.4 0.0 copy-done.3
  89.4 0.3 fusion.2
  89.7 0.8 dynamic_slice.21
  90.4 0.1 collective-permute-done
  90.6 6.6 %all-to-all-done.1 = bf16[4,48,1792]{2,1,0:T(8,128)(2,1)S(1)} async-done(((bf16[4,48,1792]{2,1,0:T(8,128)(2,1)}), bf16[4,48,1792]{2,1,0:T(8,128)(2,1)S(1)}, u32[]{:S(2)}, u32[]{:S(2)}) %all-to-all-start.1) | async-done | bytes 688160 | tf_op jit(solution)/shard_map/all_to_all | solution.py:70
  97.2 0.1 convert_reduce_fusion.1
  97.3 0.6 fusion.13
  97.9 0.2 rev.4
  98.2 0.7 all_to_all.18
  98.9 8.8 %all-to-all-start.2 = ((f32[16,1,944]{2,1,0:T(1,128)}), f32[16,1,944]{2,1,0:T(1,128)S(1)}, u32[]{:S(2)}, u32[]{:S(2)}) async-start(f32[16,1,944]{2,1,0:T(1,128)} %all_to_all.18), calls=%async_computation.2 | async-start | bytes 131072 | tf_op jit(solution)/shard_map/all_to_all | solution.py:96
  107.7 6.7 %all-to-all-done.2 = f32[16,1,944]{2,1,0:T(1,128)S(1)} async-done(((f32[16,1,944]{2,1,0:T(1,128)}), f32[16,1,944]{2,1,0:T(1,128)S(1)}, u32[]{:S(2)}, u32[]{:S(2)}) %all-to-all-start.2) | async-done | bytes 60448 | tf_op jit(solution)/shard_map/all_to_all | solution.py:96
  114.5 0.1 reshape.48
  114.7 0.7 broadcast_in_dim.8
  115.4 6.8 %all-to-all-start.3 = ((f32[32,1,1280]{2,1,0:T(1,128)}), f32[32,1,1280]{2,1,0:T(1,128)S(1)}, u32[]{:S(2)}, u32[]{:S(2)}) async-start(f32[32,1,1280]{2,1,0:T(1,128)} %broadcast_in_dim.8), calls=%async_computation.3 | async-start | bytes 327680 | tf_op jit(solution)/shard_map/all_to_all | solution.py:25
  122.2 11.3 %all-to-all-done.3 = f32[32,1,1280]{2,1,0:T(1,128)S(1)} async-done(((f32[32,1,1280]{2,1,0:T(1,128)}), f32[32,1,1280]{2,1,0:T(1,128)S(1)}, u32[]{:S(2)}, u32[]{:S(2)}) %all-to-all-start.3) | async-done | bytes 163872 | tf_op jit(solution)/shard_map/all_to_all | solution.py:25
  133.5 0.4 reduce.2
  134.0 0.6 broadcast_multiply_fusion.1
  134.6 0.6 broadcast_multiply_fusion
  (28 shorter events, 0.4 us)
Async XLA Ops:
  0.6 1.3 copy-start
  3.2 4.3 %collective-permute-start.1 = (f16[192,2048]{1,0:T(8,128)(2,1)S(1)}, f16[192,2048]{1,0:T(8,128)(2,1)S(1)}, u32[]{:S(2)}, u32[]{:S(2)}) collective-permute-start(f16[192,2048]{1,0:T(8,128)(2,1)S(1)} %fusion), channel_id=1, source_target_pairs={{0,16},{16,0},{1,17},{17,1},{2,18},{18,2},{3,19},{19,3},{4,20},{20... | collective-permute-start | bytes 2359304 | tf_op jit(solution)/shard_map/ppermute | solution.py:21
  5.1 72.4 %collective-permute-start.3 = (bf16[896,2048]{1,0:T(8,128)(2,1)}, bf16[896,2048]{1,0:T(8,128)(2,1)S(1)}, u32[]{:S(2)}, u32[]{:S(2)}) collective-permute-start(bf16[896,2048]{1,0:T(8,128)(2,1)} %param.9), channel_id=1, source_target_pairs={{0,16},{16,0},{1,17},{17,1},{2,18},{18,2},{3,19},{19,3},{4,20},{20... | collective-permute-start | bytes 11010056 | tf_op jit(solution)/shard_map/ppermute | solution.py:21
  8.0 69.5 %copy-start.4 = (bf16[896,2048]{1,0:T(8,128)(2,1)S(1)}, bf16[896,2048]{1,0:T(8,128)(2,1)}, u32[]{:S(2)}) copy-start(bf16[896,2048]{1,0:T(8,128)(2,1)} %param.9) | copy-start | bytes 11010052
  39.1 10.6 %collective-permute-start.2 = (f16[24,2048]{1,0:T(8,128)(2,1)S(1)}, f16[24,2048]{1,0:T(8,128)(2,1)S(1)}, u32[]{:S(2)}, u32[]{:S(2)}) collective-permute-start(f16[24,2048]{1,0:T(8,128)(2,1)S(1)} %multiply_convert_fusion.1), channel_id=1, source_target_pairs={{0,32},{32,0},{1,33},{33,1},{2,34},{34,2},{3,35},{35,3},{4,36},{36... | collective-permute-start | bytes 294920 | tf_op jit(solution)/shard_map/ppermute | solution.py:21
  80.2 7.2 %copy-start.1 = (s32[896]{0:T(1024)S(1)}, s32[896]{0:T(1024)}, u32[]{:S(2)}) copy-start(s32[896]{0:T(1024)} %param.13) | copy-start | bytes 10756
  80.2 7.2 %copy-start.2 = (s32[896]{0:T(1024)S(1)}, s32[896]{0:T(1024)}, u32[]{:S(2)}) copy-start(s32[896]{0:T(1024)} %param.11) | copy-start | bytes 10756
  80.3 9.1 %copy-start.3 = (s32[256,2]{0,1:T(2,128)S(1)}, s32[256,2]{0,1:T(2,128)}, u32[]{:S(2)}) copy-start(s32[256,2]{0,1:T(2,128)} %param.12) | copy-start | bytes 6148
  81.2 16.0 %all-to-all-start.1 = ((bf16[4,48,1792]{2,1,0:T(8,128)(2,1)}), bf16[4,48,1792]{2,1,0:T(8,128)(2,1)S(1)}, u32[]{:S(2)}, u32[]{:S(2)}) async-start(bf16[4,48,1792]{2,1,0:T(8,128)(2,1)} %bitcast.3), calls=%async_computation.1 | async-start | bytes 1376256 | tf_op jit(solution)/shard_map/all_to_all | solution.py:70
  87.5 3.1 %collective-permute-start = (s32[2,896]{1,0:T(2,128)S(1)}, s32[2,896]{1,0:T(2,128)S(1)}, u32[]{:S(2)}, u32[]{:S(2)}) collective-permute-start(s32[2,896]{1,0:T(2,128)S(1)} %pad_add_fusion.1), channel_id=1, source_target_pairs={{0,16},{16,0},{1,17},{17,1},{2,18},{18,2},{3,19},{19,3},{4,20},{20... | collective-permute-start | bytes 21512 | tf_op jit(solution)/shard_map/ppermute | solution.py:21
  98.9 15.6 %all-to-all-start.2 = ((f32[16,1,944]{2,1,0:T(1,128)}), f32[16,1,944]{2,1,0:T(1,128)S(1)}, u32[]{:S(2)}, u32[]{:S(2)}) async-start(f32[16,1,944]{2,1,0:T(1,128)} %all_to_all.18), calls=%async_computation.2 | async-start | bytes 131072 | tf_op jit(solution)/shard_map/all_to_all | solution.py:96
  115.4 18.1 %all-to-all-start.3 = ((f32[32,1,1280]{2,1,0:T(1,128)}), f32[32,1,1280]{2,1,0:T(1,128)S(1)}, u32[]{:S(2)}, u32[]{:S(2)}) async-start(f32[32,1,1280]{2,1,0:T(1,128)} %broadcast_in_dim.8), calls=%async_computation.3 | async-start | bytes 327680 | tf_op jit(solution)/shard_map/all_to_all | solution.py:25

commit v6 on v5

--- a/solution.py
+++ b/solution.py
@@ -50,7 +50,7 @@
     ids = jnp.concatenate([ids, other(ids, "c")], axis=1)
     part = jnp.dot(mine, precond, preferred_element_type=F32) + theirs.astype(F32) * (1.0 / (CORES * up))
     pieces = (part * up).astype(F16).reshape(n_z, half // n_z, width)
-    lines = [[CORES * i for i in range(n_z)], [CORES * i + 1 for i in reversed(range(n_z))]]
+    lines = [[(i + c * n_z // 2) % n_z * CORES + c for i in range(n_z)] for c in range(CORES)]
     pieces = lax.all_to_all(pieces, ("z", "c"), 0, 0, axis_index_groups=lines)
     block = jnp.sum(pieces.astype(F32), axis=0)
     sent = (block * (1.0 / n_z)).astype(F16)

time: 136 us -> 135 us (level)
  no operation moved by 1% of the time
where the time goes in v6:
time: 135 us
  blocking collectives  58.6 us (43%)
  starting transfers between devices  34.7 us (26%)
  waiting for transfers between devices  28.5 us (21%)
  matrix products  5.3 us (4%)
  local copies, waits for them, and re-layouts  3.99 us (3%)
  other arithmetic  2.88 us (2%)
    all_to_all x1, blocking collectives, body(): pieces = lax.all_to_all(pieces, ('z', 'c'), 0, 0, axis_index_groups=lines)  31.6 us
    all_gather x1, blocking collectives, body(): lax.all_gather(block.astype(BF16), ('z', 'c'), axis=0, tiled=True, axis_i...  27.1 us
    ppermute x4, starting transfers between devices, other(): return lax.ppermute(x, axis, [(i, i ^ step) for i in range(n)])  13.1 us
    all_to_all x1, waiting for transfers between devices, to_all(): return lax.all_to_all(jnp.broadcast_to(x[None], (n,) + x.shape), axes, 0, 0)  11.3 us
    all_to_all x1, starting transfers between devices, body(): lax.all_to_all(both.reshape(Y_PARTS * n_cf, samples + rows), ('yh', 'c',...  8.75 us
    all_to_all x1, waiting for transfers between devices, body(): lax.all_to_all(both.reshape(Y_PARTS * n_cf, samples + rows), ('yh', 'c',...  6.74 us
    all_to_all x1, starting transfers between devices, to_all(): return lax.all_to_all(jnp.broadcast_to(x[None], (n,) + x.shape), axes, 0, 0)  6.72 us
    all_to_all x1, waiting for transfers between devices, body(): lax.all_to_all(score.reshape(n_f, rows, 2 * samples), ('c', 'feat'), 0, 0...  6.59 us
  transfers between devices with their start and end apart: 7, of which 5 were waited for; matrix products, arithmetic and copies ran while one was open for 1% of the time, Pallas kernels for 0%

profile of v6, /device:TPU:8, one launch (start us, length us, event | category | flops | bytes accessed | tf_op | source)
XLA Modules:
  0.0 135.0 jit_solution(17092659715087334982)
XLA Ops:
  0.6 0.0 copy-start
  0.7 1.0 constant_dynamic-slice_fusion.1
  1.6 0.3 copy-done
  1.9 1.3 fusion
  3.2 1.9 %collective-permute-start.1 = (f16[192,2048]{1,0:T(8,128)(2,1)S(1)}, f16[192,2048]{1,0:T(8,128)(2,1)S(1)}, u32[]{:S(2)}, u32[]{:S(2)}) collective-permute-start(f16[192,2048]{1,0:T(8,128)(2,1)S(1)} %fusion), channel_id=1, source_target_pairs={{0,16},{16,0},{1,17},{17,1},{2,18},{18,2},{3,19},{19,3},{4,20},{20... | collective-permute-start | bytes 2359304 | tf_op jit(solution)/shard_map/ppermute | solution.py:21
  5.1 2.4 %collective-permute-start.3 = (bf16[896,2048]{1,0:T(8,128)(2,1)}, bf16[896,2048]{1,0:T(8,128)(2,1)S(1)}, u32[]{:S(2)}, u32[]{:S(2)}) collective-permute-start(bf16[896,2048]{1,0:T(8,128)(2,1)} %param.9), channel_id=1, source_target_pairs={{0,16},{16,0},{1,17},{17,1},{2,18},{18,2},{3,19},{19,3},{4,20},{20... | collective-permute-start | bytes 11010056 | tf_op jit(solution)/shard_map/ppermute | solution.py:21
  7.5 0.0 collective-permute-done.1
  7.5 0.5 multiply_convert_fusion
  8.0 0.0 copy-start.4
  8.0 31.6 %all_to_all.25 = f16[8,24,2048]{2,1,0:T(8,128)(2,1)S(1)} all-to-all(f16[8,24,2048]{2,1,0:T(8,128)(2,1)S(1)} %bitcast.22), channel_id=1, replica_groups={{0,64,128,192,256,320,384,448},{272,336,400,464,16,80,144,208},{1,65,12..., dimensions={0} | all-to-all | bytes 1572864 | tf_op jit(solution)/shard_map/all_to_all | solution.py:54
  39.6 0.1 convert_reduce_fusion
  39.7 6.8 %collective-permute-start.2 = (f16[24,2048]{1,0:T(8,128)(2,1)S(1)}, f16[24,2048]{1,0:T(8,128)(2,1)S(1)}, u32[]{:S(2)}, u32[]{:S(2)}) collective-permute-start(f16[24,2048]{1,0:T(8,128)(2,1)S(1)} %multiply_convert_fusion.1), channel_id=1, source_target_pairs={{0,32},{32,0},{1,33},{33,1},{2,34},{34,2},{3,35},{35,3},{4,36},{36... | collective-permute-start | bytes 294920 | tf_op jit(solution)/shard_map/ppermute | solution.py:21
  46.6 3.7 %collective-permute-done.2 = f16[24,2048]{1,0:T(8,128)(2,1)S(1)} collective-permute-done((f16[24,2048]{1,0:T(8,128)(2,1)S(1)}, f16[24,2048]{1,0:T(8,128)(2,1)S(1)}, u32[]{:S(2)}, u32[]{:S(2)}) %collective-permute-start.2) | collective-permute-done | bytes 98336 | tf_op jit(solution)/shard_map/ppermute | solution.py:21
  50.3 27.1 %all_gather.3 = bf16[192,2048]{1,0:T(8,128)(2,1)S(1)} all-gather(bf16[24,2048]{1,0:T(8,128)(2,1)S(1)} %add_convert_fusion), channel_id=1, replica_groups={{0,64,128,192,256,320,384,448},{272,336,400,464,16,80,144,208},{1,65,12..., dimensions={0}, use_global_device_ids=true | all-gather | bytes 884736 | tf_op jit(solution)/shard_map/all_gather | solution.py:58
  77.4 0.0 collective-permute-done.3
  77.4 0.0 copy-done.4
  77.4 1.4 %convolution_convert_fusion.1 = bf16[192,896]{1,0:T(8,128)(2,1)S(1)} fusion(bf16[192,2048]{1,0:T(8,128)(2,1)S(1)} %all_gather.3, bf16[896,2048]{1,0:T(8,128)(2,1)S(1)} %copy-done.4), kind=kOutput, calls=%fused_computation.8 | convolution fusion | flops 704815104 | bytes 4800512 | tf_op jit(solution)/shard_map/dot_general | solution.py:64
  78.8 1.4 %convolution_convert_fusion = bf16[192,896]{1,0:T(8,128)(2,1)S(1)} fusion(bf16[192,2048]{1,0:T(8,128)(2,1)S(1)} %all_gather.3, bf16[896,2048]{1,0:T(8,128)(2,1)S(1)} %collective-permute-done.3), kind=kOutput, calls=%fused_computation.7 | convolution fusion | flops 704815104 | bytes 4800512 | tf_op jit(solution)/shard_map/dot_general | solution.py:65
  80.1 0.0 copy-start.1
  80.2 0.0 copy-start.2
  80.2 0.0 copy-start.3
  80.2 0.9 pad_maximum_fusion
  81.1 6.2 %all-to-all-start.1 = ((bf16[4,48,1792]{2,1,0:T(8,128)(2,1)}), bf16[4,48,1792]{2,1,0:T(8,128)(2,1)S(1)}, u32[]{:S(2)}, u32[]{:S(2)}) async-start(bf16[4,48,1792]{2,1,0:T(8,128)(2,1)} %bitcast.3), calls=%async_computation.1 | async-start | bytes 1376256 | tf_op jit(solution)/shard_map/all_to_all | solution.py:70
  87.3 0.0 copy-done.1
  87.3 0.0 copy-done.2
  87.3 1.9 %collective-permute-start = (s32[2,896]{1,0:T(2,128)S(1)}, s32[2,896]{1,0:T(2,128)S(1)}, u32[]{:S(2)}, u32[]{:S(2)}) collective-permute-start(s32[2,896]{1,0:T(2,128)S(1)} %pad_add_fusion.1), channel_id=1, source_target_pairs={{0,16},{16,0},{1,17},{17,1},{2,18},{18,2},{3,19},{19,3},{4,20},{20... | collective-permute-start | bytes 21512 | tf_op jit(solution)/shard_map/ppermute | solution.py:21
  89.3 0.0 copy-done.3
  89.3 0.3 fusion.2
  89.6 0.8 dynamic_slice.21
  90.3 0.1 collective-permute-done
  90.5 6.6 %all-to-all-done.1 = bf16[4,48,1792]{2,1,0:T(8,128)(2,1)S(1)} async-done(((bf16[4,48,1792]{2,1,0:T(8,128)(2,1)}), bf16[4,48,1792]{2,1,0:T(8,128)(2,1)S(1)}, u32[]{:S(2)}, u32[]{:S(2)}) %all-to-all-start.1) | async-done | bytes 688160 | tf_op jit(solution)/shard_map/all_to_all | solution.py:70
  97.1 0.1 convert_reduce_fusion.1
  97.2 0.6 fusion.13
  97.8 0.2 rev.4
  98.0 0.7 all_to_all.18
  98.8 8.7 %all-to-all-start.2 = ((f32[16,1,944]{2,1,0:T(1,128)}), f32[16,1,944]{2,1,0:T(1,128)S(1)}, u32[]{:S(2)}, u32[]{:S(2)}) async-start(f32[16,1,944]{2,1,0:T(1,128)} %all_to_all.18), calls=%async_computation.2 | async-start | bytes 131072 | tf_op jit(solution)/shard_map/all_to_all | solution.py:96
  107.5 6.7 %all-to-all-done.2 = f32[16,1,944]{2,1,0:T(1,128)S(1)} async-done(((f32[16,1,944]{2,1,0:T(1,128)}), f32[16,1,944]{2,1,0:T(1,128)S(1)}, u32[]{:S(2)}, u32[]{:S(2)}) %all-to-all-start.2) | async-done | bytes 60448 | tf_op jit(solution)/shard_map/all_to_all | solution.py:96
  114.3 0.1 reshape.48
  114.4 0.7 broadcast_in_dim.8
  115.2 6.7 %all-to-all-start.3 = ((f32[32,1,1280]{2,1,0:T(1,128)}), f32[32,1,1280]{2,1,0:T(1,128)S(1)}, u32[]{:S(2)}, u32[]{:S(2)}) async-start(f32[32,1,1280]{2,1,0:T(1,128)} %broadcast_in_dim.8), calls=%async_computation.3 | async-start | bytes 327680 | tf_op jit(solution)/shard_map/all_to_all | solution.py:25
  121.9 11.3 %all-to-all-done.3 = f32[32,1,1280]{2,1,0:T(1,128)S(1)} async-done(((f32[32,1,1280]{2,1,0:T(1,128)}), f32[32,1,1280]{2,1,0:T(1,128)S(1)}, u32[]{:S(2)}, u32[]{:S(2)}) %all-to-all-start.3) | async-done | bytes 163872 | tf_op jit(solution)/shard_map/all_to_all | solution.py:25
  133.2 0.4 reduce.2
  133.8 0.6 broadcast_multiply_fusion.1
  134.4 0.6 broadcast_multiply_fusion
  (28 shorter events, 0.4 us)
Async XLA Ops:
  0.6 1.3 copy-start
  3.2 4.3 %collective-permute-start.1 = (f16[192,2048]{1,0:T(8,128)(2,1)S(1)}, f16[192,2048]{1,0:T(8,128)(2,1)S(1)}, u32[]{:S(2)}, u32[]{:S(2)}) collective-permute-start(f16[192,2048]{1,0:T(8,128)(2,1)S(1)} %fusion), channel_id=1, source_target_pairs={{0,16},{16,0},{1,17},{17,1},{2,18},{18,2},{3,19},{19,3},{4,20},{20... | collective-permute-start | bytes 2359304 | tf_op jit(solution)/shard_map/ppermute | solution.py:21
  5.1 72.3 %collective-permute-start.3 = (bf16[896,2048]{1,0:T(8,128)(2,1)}, bf16[896,2048]{1,0:T(8,128)(2,1)S(1)}, u32[]{:S(2)}, u32[]{:S(2)}) collective-permute-start(bf16[896,2048]{1,0:T(8,128)(2,1)} %param.9), channel_id=1, source_target_pairs={{0,16},{16,0},{1,17},{17,1},{2,18},{18,2},{3,19},{19,3},{4,20},{20... | collective-permute-start | bytes 11010056 | tf_op jit(solution)/shard_map/ppermute | solution.py:21
  8.0 69.4 %copy-start.4 = (bf16[896,2048]{1,0:T(8,128)(2,1)S(1)}, bf16[896,2048]{1,0:T(8,128)(2,1)}, u32[]{:S(2)}) copy-start(bf16[896,2048]{1,0:T(8,128)(2,1)} %param.9) | copy-start | bytes 11010052
  39.7 10.6 %collective-permute-start.2 = (f16[24,2048]{1,0:T(8,128)(2,1)S(1)}, f16[24,2048]{1,0:T(8,128)(2,1)S(1)}, u32[]{:S(2)}, u32[]{:S(2)}) collective-permute-start(f16[24,2048]{1,0:T(8,128)(2,1)S(1)} %multiply_convert_fusion.1), channel_id=1, source_target_pairs={{0,32},{32,0},{1,33},{33,1},{2,34},{34,2},{3,35},{35,3},{4,36},{36... | collective-permute-start | bytes 294920 | tf_op jit(solution)/shard_map/ppermute | solution.py:21
  80.1 7.1 %copy-start.1 = (s32[896]{0:T(1024)S(1)}, s32[896]{0:T(1024)}, u32[]{:S(2)}) copy-start(s32[896]{0:T(1024)} %param.13) | copy-start | bytes 10756
  80.2 7.1 %copy-start.2 = (s32[896]{0:T(1024)S(1)}, s32[896]{0:T(1024)}, u32[]{:S(2)}) copy-start(s32[896]{0:T(1024)} %param.11) | copy-start | bytes 10756
  80.2 9.1 %copy-start.3 = (s32[256,2]{0,1:T(2,128)S(1)}, s32[256,2]{0,1:T(2,128)}, u32[]{:S(2)}) copy-start(s32[256,2]{0,1:T(2,128)} %param.12) | copy-start | bytes 6148
  81.1 16.0 %all-to-all-start.1 = ((bf16[4,48,1792]{2,1,0:T(8,128)(2,1)}), bf16[4,48,1792]{2,1,0:T(8,128)(2,1)S(1)}, u32[]{:S(2)}, u32[]{:S(2)}) async-start(bf16[4,48,1792]{2,1,0:T(8,128)(2,1)} %bitcast.3), calls=%async_computation.1 | async-start | bytes 1376256 | tf_op jit(solution)/shard_map/all_to_all | solution.py:70
  87.3 3.1 %collective-permute-start = (s32[2,896]{1,0:T(2,128)S(1)}, s32[2,896]{1,0:T(2,128)S(1)}, u32[]{:S(2)}, u32[]{:S(2)}) collective-permute-start(s32[2,896]{1,0:T(2,128)S(1)} %pad_add_fusion.1), channel_id=1, source_target_pairs={{0,16},{16,0},{1,17},{17,1},{2,18},{18,2},{3,19},{19,3},{4,20},{20... | collective-permute-start | bytes 21512 | tf_op jit(solution)/shard_map/ppermute | solution.py:21
  98.8 15.5 %all-to-all-start.2 = ((f32[16,1,944]{2,1,0:T(1,128)}), f32[16,1,944]{2,1,0:T(1,128)S(1)}, u32[]{:S(2)}, u32[]{:S(2)}) async-start(f32[16,1,944]{2,1,0:T(1,128)} %all_to_all.18), calls=%async_computation.2 | async-start | bytes 131072 | tf_op jit(solution)/shard_map/all_to_all | solution.py:96
  115.2 18.1 %all-to-all-start.3 = ((f32[32,1,1280]{2,1,0:T(1,128)}), f32[32,1,1280]{2,1,0:T(1,128)S(1)}, u32[]{:S(2)}, u32[]{:S(2)}) async-start(f32[32,1,1280]{2,1,0:T(1,128)} %broadcast_in_dim.8), calls=%async_computation.3 | async-start | bytes 327680 | tf_op jit(solution)/shard_map/all_to_all | solution.py:25

commit v7 on v6

--- a/solution.py
+++ b/solution.py
@@ -29,7 +29,8 @@
     n_z, n_f, n_q = lax.axis_size("z"), lax.axis_size("feat"), lax.axis_size("query")
     n_t = n_z * Y_PARTS
     core = lax.axis_index("c")
-    lane = jnp.where(core == 0, lax.axis_index("feat"), n_f - 1 - lax.axis_index("feat"))
+    turn = n_f // 2
+    lane = lax.rem(lax.axis_index("feat") + core * (n_f - turn), n_f)
     query_rows, depth = queries.shape
     width = precond.shape[1]
     samples = train_feats.shape[0]
@@ -66,7 +67,7 @@
         ],
         axis=1,
     )
-    lanes = [list(range(n_f)), [n_f + i for i in reversed(range(n_f))]]
+    lanes = [[c * n_f + (i + c * turn) % n_f for i in range(n_f)] for c in range(CORES)]
     score = lax.all_to_all(score.reshape(n_f, rows, 2 * samples), ("c", "feat"), 0, 0, axis_index_groups=lanes)
     score = jnp.sum(score.astype(F32), axis=0) * float(feat) ** (-0.5)
 
@@ -96,7 +97,7 @@
     both = lax.all_to_all(both.reshape(Y_PARTS * n_cf, samples + rows), ("yh", "c", "feat"), 0, 0)
     both = both.reshape(Y_PARTS, n_cf, samples + rows)
     by_query = jnp.sum(both[:, :, samples:], axis=0).reshape(CORES, n_f, rows)
-    by_query = jnp.concatenate([by_query[0], by_query[1, ::-1]]).reshape(query_rows)
+    by_query = jnp.concatenate([by_query[0], by_query[1, turn:], by_query[1, :turn]]).reshape(query_rows)
     by_sample = lax.dynamic_index_in_dim(both, lax.axis_index("yh"), 0, False)[:, :samples]
     by_sample = jnp.sum(by_sample, axis=0)
 

time: 135 us -> 135 us (level)
  no operation moved by 1% of the time
where the time goes in v7:
time: 135 us
  blocking collectives  58.6 us (43%)
  starting transfers between devices  34.7 us (26%)
  waiting for transfers between devices  28.5 us (21%)
  matrix products  5.3 us (4%)
  local copies, waits for them, and re-layouts  3.96 us (3%)
  other arithmetic  2.88 us (2%)
    all_to_all x1, blocking collectives, body(): pieces = lax.all_to_all(pieces, ('z', 'c'), 0, 0, axis_index_groups=lines)  31.6 us
    all_gather x1, blocking collectives, body(): lax.all_gather(block.astype(BF16), ('z', 'c'), axis=0, tiled=True, axis_i...  27.1 us
    ppermute x4, starting transfers between devices, other(): return lax.ppermute(x, axis, [(i, i ^ step) for i in range(n)])  13.1 us
    all_to_all x1, waiting for transfers between devices, to_all(): return lax.all_to_all(jnp.broadcast_to(x[None], (n,) + x.shape), axes, 0, 0)  11.3 us
    all_to_all x1, starting transfers between devices, body(): lax.all_to_all(both.reshape(Y_PARTS * n_cf, samples + rows), ('yh', 'c',...  8.68 us
    all_to_all x1, waiting for transfers between devices, body(): lax.all_to_all(both.reshape(Y_PARTS * n_cf, samples + rows), ('yh', 'c',...  6.74 us
    all_to_all x1, starting transfers between devices, to_all(): return lax.all_to_all(jnp.broadcast_to(x[None], (n,) + x.shape), axes, 0, 0)  6.72 us
    all_to_all x1, waiting for transfers between devices, body(): lax.all_to_all(score.reshape(n_f, rows, 2 * samples), ('c', 'feat'), 0, 0...  6.66 us
  transfers between devices with their start and end apart: 7, of which 5 were waited for; matrix products, arithmetic and copies ran while one was open for 1% of the time, Pallas kernels for 0%

profile of v7, /device:TPU:8, one launch (start us, length us, event | category | flops | bytes accessed | tf_op | source)
XLA Modules:
  0.0 134.9 jit_solution(12582399267363802195)
XLA Ops:
  0.6 0.0 copy-start
  0.7 1.0 constant_dynamic-slice_fusion.1
  1.6 0.3 copy-done
  1.9 1.3 fusion
  3.2 1.9 %collective-permute-start.1 = (f16[192,2048]{1,0:T(8,128)(2,1)S(1)}, f16[192,2048]{1,0:T(8,128)(2,1)S(1)}, u32[]{:S(2)}, u32[]{:S(2)}) collective-permute-start(f16[192,2048]{1,0:T(8,128)(2,1)S(1)} %fusion), channel_id=1, source_target_pairs={{0,16},{16,0},{1,17},{17,1},{2,18},{18,2},{3,19},{19,3},{4,20},{20... | collective-permute-start | bytes 2359304 | tf_op jit(solution)/shard_map/ppermute | solution.py:21
  5.1 2.4 %collective-permute-start.3 = (bf16[896,2048]{1,0:T(8,128)(2,1)}, bf16[896,2048]{1,0:T(8,128)(2,1)S(1)}, u32[]{:S(2)}, u32[]{:S(2)}) collective-permute-start(bf16[896,2048]{1,0:T(8,128)(2,1)} %param.9), channel_id=1, source_target_pairs={{0,16},{16,0},{1,17},{17,1},{2,18},{18,2},{3,19},{19,3},{4,20},{20... | collective-permute-start | bytes 11010056 | tf_op jit(solution)/shard_map/ppermute | solution.py:21
  7.5 0.0 collective-permute-done.1
  7.5 0.5 multiply_convert_fusion
  8.0 0.0 copy-start.4
  8.0 31.6 %all_to_all.25 = f16[8,24,2048]{2,1,0:T(8,128)(2,1)S(1)} all-to-all(f16[8,24,2048]{2,1,0:T(8,128)(2,1)S(1)} %bitcast.27), channel_id=1, replica_groups={{0,64,128,192,256,320,384,448},{272,336,400,464,16,80,144,208},{1,65,12..., dimensions={0} | all-to-all | bytes 1572864 | tf_op jit(solution)/shard_map/all_to_all | solution.py:55
  39.6 0.1 convert_reduce_fusion
  39.7 6.8 %collective-permute-start.2 = (f16[24,2048]{1,0:T(8,128)(2,1)S(1)}, f16[24,2048]{1,0:T(8,128)(2,1)S(1)}, u32[]{:S(2)}, u32[]{:S(2)}) collective-permute-start(f16[24,2048]{1,0:T(8,128)(2,1)S(1)} %multiply_convert_fusion.1), channel_id=1, source_target_pairs={{0,32},{32,0},{1,33},{33,1},{2,34},{34,2},{3,35},{35,3},{4,36},{36... | collective-permute-start | bytes 294920 | tf_op jit(solution)/shard_map/ppermute | solution.py:21
  46.6 3.7 %collective-permute-done.2 = f16[24,2048]{1,0:T(8,128)(2,1)S(1)} collective-permute-done((f16[24,2048]{1,0:T(8,128)(2,1)S(1)}, f16[24,2048]{1,0:T(8,128)(2,1)S(1)}, u32[]{:S(2)}, u32[]{:S(2)}) %collective-permute-start.2) | collective-permute-done | bytes 98336 | tf_op jit(solution)/shard_map/ppermute | solution.py:21
  50.3 27.1 %all_gather.3 = bf16[192,2048]{1,0:T(8,128)(2,1)S(1)} all-gather(bf16[24,2048]{1,0:T(8,128)(2,1)S(1)} %add_convert_fusion), channel_id=1, replica_groups={{0,64,128,192,256,320,384,448},{272,336,400,464,16,80,144,208},{1,65,12..., dimensions={0}, use_global_device_ids=true | all-gather | bytes 884736 | tf_op jit(solution)/shard_map/all_gather | solution.py:59
  77.4 0.0 collective-permute-done.3
  77.4 0.0 copy-done.4
  77.4 1.4 %convolution_convert_fusion.1 = bf16[192,896]{1,0:T(8,128)(2,1)S(1)} fusion(bf16[192,2048]{1,0:T(8,128)(2,1)S(1)} %all_gather.3, bf16[896,2048]{1,0:T(8,128)(2,1)S(1)} %copy-done.4), kind=kOutput, calls=%fused_computation.8 | convolution fusion | flops 704815104 | bytes 4800512 | tf_op jit(solution)/shard_map/dot_general | solution.py:65
  78.8 1.4 %convolution_convert_fusion = bf16[192,896]{1,0:T(8,128)(2,1)S(1)} fusion(bf16[192,2048]{1,0:T(8,128)(2,1)S(1)} %all_gather.3, bf16[896,2048]{1,0:T(8,128)(2,1)S(1)} %collective-permute-done.3), kind=kOutput, calls=%fused_computation.7 | convolution fusion | flops 704815104 | bytes 4800512 | tf_op jit(solution)/shard_map/dot_general | solution.py:66
  80.1 0.0 copy-start.1
  80.2 0.0 copy-start.2
  80.2 0.0 copy-start.3
  80.2 0.9 pad_maximum_fusion
  81.1 6.2 %all-to-all-start.1 = ((bf16[4,48,1792]{2,1,0:T(8,128)(2,1)}), bf16[4,48,1792]{2,1,0:T(8,128)(2,1)S(1)}, u32[]{:S(2)}, u32[]{:S(2)}) async-start(bf16[4,48,1792]{2,1,0:T(8,128)(2,1)} %bitcast.3), calls=%async_computation.1 | async-start | bytes 1376256 | tf_op jit(solution)/shard_map/all_to_all | solution.py:71
  87.3 0.0 copy-done.1
  87.3 0.0 copy-done.2
  87.3 1.9 %collective-permute-start = (s32[2,896]{1,0:T(2,128)S(1)}, s32[2,896]{1,0:T(2,128)S(1)}, u32[]{:S(2)}, u32[]{:S(2)}) collective-permute-start(s32[2,896]{1,0:T(2,128)S(1)} %pad_add_fusion.1), channel_id=1, source_target_pairs={{0,16},{16,0},{1,17},{17,1},{2,18},{18,2},{3,19},{19,3},{4,20},{20... | collective-permute-start | bytes 21512 | tf_op jit(solution)/shard_map/ppermute | solution.py:21
  89.3 0.0 copy-done.3
  89.3 0.3 fusion.2
  89.6 0.8 dynamic_slice.21
  90.3 0.1 collective-permute-done
  90.5 6.7 %all-to-all-done.1 = bf16[4,48,1792]{2,1,0:T(8,128)(2,1)S(1)} async-done(((bf16[4,48,1792]{2,1,0:T(8,128)(2,1)}), bf16[4,48,1792]{2,1,0:T(8,128)(2,1)S(1)}, u32[]{:S(2)}, u32[]{:S(2)}) %all-to-all-start.1) | async-done | bytes 688160 | tf_op jit(solution)/shard_map/all_to_all | solution.py:71
  97.1 0.1 convert_reduce_fusion.1
  97.2 0.6 fusion.13
  97.8 0.2 rev.3
  98.1 0.7 all_to_all.18
  98.8 8.7 %all-to-all-start.2 = ((f32[16,1,944]{2,1,0:T(1,128)}), f32[16,1,944]{2,1,0:T(1,128)S(1)}, u32[]{:S(2)}, u32[]{:S(2)}) async-start(f32[16,1,944]{2,1,0:T(1,128)} %all_to_all.18), calls=%async_computation.2 | async-start | bytes 131072 | tf_op jit(solution)/shard_map/all_to_all | solution.py:97
  107.5 6.7 %all-to-all-done.2 = f32[16,1,944]{2,1,0:T(1,128)S(1)} async-done(((f32[16,1,944]{2,1,0:T(1,128)}), f32[16,1,944]{2,1,0:T(1,128)S(1)}, u32[]{:S(2)}, u32[]{:S(2)}) %all-to-all-start.2) | async-done | bytes 60448 | tf_op jit(solution)/shard_map/all_to_all | solution.py:97
  114.3 0.1 reshape.48
  114.4 0.7 broadcast_in_dim.8
  115.2 6.7 %all-to-all-start.3 = ((f32[32,1,1280]{2,1,0:T(1,128)}), f32[32,1,1280]{2,1,0:T(1,128)S(1)}, u32[]{:S(2)}, u32[]{:S(2)}) async-start(f32[32,1,1280]{2,1,0:T(1,128)} %broadcast_in_dim.8), calls=%async_computation.3 | async-start | bytes 327680 | tf_op jit(solution)/shard_map/all_to_all | solution.py:25
  121.9 11.3 %all-to-all-done.3 = f32[32,1,1280]{2,1,0:T(1,128)S(1)} async-done(((f32[32,1,1280]{2,1,0:T(1,128)}), f32[32,1,1280]{2,1,0:T(1,128)S(1)}, u32[]{:S(2)}, u32[]{:S(2)}) %all-to-all-start.3) | async-done | bytes 163872 | tf_op jit(solution)/shard_map/all_to_all | solution.py:25
  133.2 0.4 reduce.2
  133.7 0.6 broadcast_multiply_fusion.1
  134.4 0.6 broadcast_multiply_fusion
  (28 shorter events, 0.4 us)
Async XLA Ops:
  0.6 1.3 copy-start
  3.2 4.3 %collective-permute-start.1 = (f16[192,2048]{1,0:T(8,128)(2,1)S(1)}, f16[192,2048]{1,0:T(8,128)(2,1)S(1)}, u32[]{:S(2)}, u32[]{:S(2)}) collective-permute-start(f16[192,2048]{1,0:T(8,128)(2,1)S(1)} %fusion), channel_id=1, source_target_pairs={{0,16},{16,0},{1,17},{17,1},{2,18},{18,2},{3,19},{19,3},{4,20},{20... | collective-permute-start | bytes 2359304 | tf_op jit(solution)/shard_map/ppermute | solution.py:21
  5.1 72.3 %collective-permute-start.3 = (bf16[896,2048]{1,0:T(8,128)(2,1)}, bf16[896,2048]{1,0:T(8,128)(2,1)S(1)}, u32[]{:S(2)}, u32[]{:S(2)}) collective-permute-start(bf16[896,2048]{1,0:T(8,128)(2,1)} %param.9), channel_id=1, source_target_pairs={{0,16},{16,0},{1,17},{17,1},{2,18},{18,2},{3,19},{19,3},{4,20},{20... | collective-permute-start | bytes 11010056 | tf_op jit(solution)/shard_map/ppermute | solution.py:21
  8.0 69.4 %copy-start.4 = (bf16[896,2048]{1,0:T(8,128)(2,1)S(1)}, bf16[896,2048]{1,0:T(8,128)(2,1)}, u32[]{:S(2)}) copy-start(bf16[896,2048]{1,0:T(8,128)(2,1)} %param.9) | copy-start | bytes 11010052
  39.7 10.6 %collective-permute-start.2 = (f16[24,2048]{1,0:T(8,128)(2,1)S(1)}, f16[24,2048]{1,0:T(8,128)(2,1)S(1)}, u32[]{:S(2)}, u32[]{:S(2)}) collective-permute-start(f16[24,2048]{1,0:T(8,128)(2,1)S(1)} %multiply_convert_fusion.1), channel_id=1, source_target_pairs={{0,32},{32,0},{1,33},{33,1},{2,34},{34,2},{3,35},{35,3},{4,36},{36... | collective-permute-start | bytes 294920 | tf_op jit(solution)/shard_map/ppermute | solution.py:21
  80.1 7.1 %copy-start.1 = (s32[896]{0:T(1024)S(1)}, s32[896]{0:T(1024)}, u32[]{:S(2)}) copy-start(s32[896]{0:T(1024)} %param.13) | copy-start | bytes 10756
  80.2 7.1 %copy-start.2 = (s32[896]{0:T(1024)S(1)}, s32[896]{0:T(1024)}, u32[]{:S(2)}) copy-start(s32[896]{0:T(1024)} %param.11) | copy-start | bytes 10756
  80.2 9.1 %copy-start.3 = (s32[256,2]{0,1:T(2,128)S(1)}, s32[256,2]{0,1:T(2,128)}, u32[]{:S(2)}) copy-start(s32[256,2]{0,1:T(2,128)} %param.12) | copy-start | bytes 6148
  81.1 16.0 %all-to-all-start.1 = ((bf16[4,48,1792]{2,1,0:T(8,128)(2,1)}), bf16[4,48,1792]{2,1,0:T(8,128)(2,1)S(1)}, u32[]{:S(2)}, u32[]{:S(2)}) async-start(bf16[4,48,1792]{2,1,0:T(8,128)(2,1)} %bitcast.3), calls=%async_computation.1 | async-start | bytes 1376256 | tf_op jit(solution)/shard_map/all_to_all | solution.py:71
  87.3 3.1 %collective-permute-start = (s32[2,896]{1,0:T(2,128)S(1)}, s32[2,896]{1,0:T(2,128)S(1)}, u32[]{:S(2)}, u32[]{:S(2)}) collective-permute-start(s32[2,896]{1,0:T(2,128)S(1)} %pad_add_fusion.1), channel_id=1, source_target_pairs={{0,16},{16,0},{1,17},{17,1},{2,18},{18,2},{3,19},{19,3},{4,20},{20... | collective-permute-start | bytes 21512 | tf_op jit(solution)/shard_map/ppermute | solution.py:21
  98.8 15.4 %all-to-all-start.2 = ((f32[16,1,944]{2,1,0:T(1,128)}), f32[16,1,944]{2,1,0:T(1,128)S(1)}, u32[]{:S(2)}, u32[]{:S(2)}) async-start(f32[16,1,944]{2,1,0:T(1,128)} %all_to_all.18), calls=%async_computation.2 | async-start | bytes 131072 | tf_op jit(solution)/shard_map/all_to_all | solution.py:97
  115.2 18.1 %all-to-all-start.3 = ((f32[32,1,1280]{2,1,0:T(1,128)}), f32[32,1,1280]{2,1,0:T(1,128)S(1)}, u32[]{:S(2)}, u32[]{:S(2)}) async-start(f32[32,1,1280]{2,1,0:T(1,128)} %broadcast_in_dim.8), calls=%async_computation.3 | async-start | bytes 327680 | tf_op jit(solution)/shard_map/all_to_all | solution.py:25

commit v8 on v7

--- a/solution.py
+++ b/solution.py
@@ -51,7 +51,7 @@
     ids = jnp.concatenate([ids, other(ids, "c")], axis=1)
     part = jnp.dot(mine, precond, preferred_element_type=F32) + theirs.astype(F32) * (1.0 / (CORES * up))
     pieces = (part * up).astype(F16).reshape(n_z, half // n_z, width)
-    lines = [[(i + c * n_z // 2) % n_z * CORES + c for i in range(n_z)] for c in range(CORES)]
+    lines = [[i * CORES for i in range(n_z)], [(n_z // 2 - 1 - i) % n_z * CORES + 1 for i in range(n_z)]]
     pieces = lax.all_to_all(pieces, ("z", "c"), 0, 0, axis_index_groups=lines)
     block = jnp.sum(pieces.astype(F32), axis=0)
     sent = (block * (1.0 / n_z)).astype(F16)

time: 135 us -> 137 us (1.015)
  waiting for transfers between devices: 28.5 us -> 30.4 us
where the time goes in v8:
time: 137 us; the launch traced here: 136 us
  blocking collectives  59.2 us (43%)
  starting transfers between devices  33.8 us (25%)
  waiting for transfers between devices  30.4 us (22%)
  matrix products  5.31 us (4%)
  local copies, waits for them, and re-layouts  3.96 us (3%)
  other arithmetic  2.88 us (2%)
    all_to_all x1, blocking collectives, body(): pieces = lax.all_to_all(pieces, ('z', 'c'), 0, 0, axis_index_groups=lines)  32.9 us
    all_gather x1, blocking collectives, body(): lax.all_gather(block.astype(BF16), ('z', 'c'), axis=0, tiled=True, axis_i...  26.3 us
    ppermute x4, starting transfers between devices, other(): return lax.ppermute(x, axis, [(i, i ^ step) for i in range(n)])  13.1 us
    all_to_all x1, waiting for transfers between devices, to_all(): return lax.all_to_all(jnp.broadcast_to(x[None], (n,) + x.shape), axes, 0, 0)  11.3 us
    all_to_all x1, starting transfers between devices, body(): lax.all_to_all(both.reshape(Y_PARTS * n_cf, samples + rows), ('yh', 'c',...  7.81 us
    all_to_all x1, starting transfers between devices, to_all(): return lax.all_to_all(jnp.broadcast_to(x[None], (n,) + x.shape), axes, 0, 0)  7.73 us
    all_to_all x1, waiting for transfers between devices, body(): lax.all_to_all(score.reshape(n_f, rows, 2 * samples), ('c', 'feat'), 0, 0...  7.55 us
    all_to_all x1, waiting for transfers between devices, body(): lax.all_to_all(both.reshape(Y_PARTS * n_cf, samples + rows), ('yh', 'c',...  6.74 us
  transfers between devices with their start and end apart: 7, of which 5 were waited for; matrix products, arithmetic and copies ran while one was open for 1% of the time, Pallas kernels for 0%

profile of v8, /device:TPU:8, one launch (start us, length us, event | category | flops | bytes accessed | tf_op | source)
XLA Modules:
  0.0 136.5 jit_solution(6099618925223982630)
XLA Ops:
  0.6 0.0 copy-start
  0.7 1.0 constant_dynamic-slice_fusion.1
  1.6 0.3 copy-done
  1.9 1.3 fusion
  3.2 1.9 %collective-permute-start.1 = (f16[192,2048]{1,0:T(8,128)(2,1)S(1)}, f16[192,2048]{1,0:T(8,128)(2,1)S(1)}, u32[]{:S(2)}, u32[]{:S(2)}) collective-permute-start(f16[192,2048]{1,0:T(8,128)(2,1)S(1)} %fusion), channel_id=1, source_target_pairs={{0,16},{16,0},{1,17},{17,1},{2,18},{18,2},{3,19},{19,3},{4,20},{20... | collective-permute-start | bytes 2359304 | tf_op jit(solution)/shard_map/ppermute | solution.py:21
  5.1 2.4 %collective-permute-start.3 = (bf16[896,2048]{1,0:T(8,128)(2,1)}, bf16[896,2048]{1,0:T(8,128)(2,1)S(1)}, u32[]{:S(2)}, u32[]{:S(2)}) collective-permute-start(bf16[896,2048]{1,0:T(8,128)(2,1)} %param.9), channel_id=1, source_target_pairs={{0,16},{16,0},{1,17},{17,1},{2,18},{18,2},{3,19},{19,3},{4,20},{20... | collective-permute-start | bytes 11010056 | tf_op jit(solution)/shard_map/ppermute | solution.py:21
  7.5 0.0 collective-permute-done.1
  7.5 0.5 multiply_convert_fusion
  8.0 0.0 copy-start.4
  8.0 32.9 %all_to_all.25 = f16[8,24,2048]{2,1,0:T(8,128)(2,1)S(1)} all-to-all(f16[8,24,2048]{2,1,0:T(8,128)(2,1)S(1)} %bitcast.27), channel_id=1, replica_groups={{0,64,128,192,256,320,384,448},{208,144,80,16,464,400,336,272},{1,65,12..., dimensions={0} | all-to-all | bytes 1572864 | tf_op jit(solution)/shard_map/all_to_all | solution.py:55
  40.9 0.1 convert_reduce_fusion
  41.0 6.8 %collective-permute-start.2 = (f16[24,2048]{1,0:T(8,128)(2,1)S(1)}, f16[24,2048]{1,0:T(8,128)(2,1)S(1)}, u32[]{:S(2)}, u32[]{:S(2)}) collective-permute-start(f16[24,2048]{1,0:T(8,128)(2,1)S(1)} %multiply_convert_fusion.1), channel_id=1, source_target_pairs={{0,32},{32,0},{1,33},{33,1},{2,34},{34,2},{3,35},{35,3},{4,36},{36... | collective-permute-start | bytes 294920 | tf_op jit(solution)/shard_map/ppermute | solution.py:21
  47.9 4.7 %collective-permute-done.2 = f16[24,2048]{1,0:T(8,128)(2,1)S(1)} collective-permute-done((f16[24,2048]{1,0:T(8,128)(2,1)S(1)}, f16[24,2048]{1,0:T(8,128)(2,1)S(1)}, u32[]{:S(2)}, u32[]{:S(2)}) %collective-permute-start.2) | collective-permute-done | bytes 98336 | tf_op jit(solution)/shard_map/ppermute | solution.py:21
  52.7 26.3 %all_gather.3 = bf16[192,2048]{1,0:T(8,128)(2,1)S(1)} all-gather(bf16[24,2048]{1,0:T(8,128)(2,1)S(1)} %add_convert_fusion), channel_id=1, replica_groups={{0,64,128,192,256,320,384,448},{208,144,80,16,464,400,336,272},{1,65,12..., dimensions={0}, use_global_device_ids=true | all-gather | bytes 884736 | tf_op jit(solution)/shard_map/all_gather | solution.py:59
  79.0 0.0 collective-permute-done.3
  79.0 0.0 copy-done.4
  79.0 1.4 convolution_convert_fusion.1
  80.3 1.4 convolution_convert_fusion
  81.7 0.0 copy-start.1
  81.7 0.0 copy-start.2
  81.7 0.0 copy-start.3
  81.7 0.9 pad_maximum_fusion
  82.7 5.1 %all-to-all-start.1 = ((bf16[4,48,1792]{2,1,0:T(8,128)(2,1)}), bf16[4,48,1792]{2,1,0:T(8,128)(2,1)S(1)}, u32[]{:S(2)}, u32[]{:S(2)}) async-start(bf16[4,48,1792]{2,1,0:T(8,128)(2,1)} %bitcast.3), calls=%async_computation.1 | async-start | bytes 1376256 | tf_op jit(solution)/shard_map/all_to_all | solution.py:71
  87.8 0.0 copy-done.1
  87.8 0.0 copy-done.2
  87.8 1.9 %collective-permute-start = (s32[2,896]{1,0:T(2,128)S(1)}, s32[2,896]{1,0:T(2,128)S(1)}, u32[]{:S(2)}, u32[]{:S(2)}) collective-permute-start(s32[2,896]{1,0:T(2,128)S(1)} %pad_add_fusion.1), channel_id=1, source_target_pairs={{0,16},{16,0},{1,17},{17,1},{2,18},{18,2},{3,19},{19,3},{4,20},{20... | collective-permute-start | bytes 21512 | tf_op jit(solution)/shard_map/ppermute | solution.py:21
  89.8 0.0 copy-done.3
  89.8 0.3 fusion.2
  90.1 0.8 dynamic_slice.21
  90.8 0.1 collective-permute-done
  91.0 7.5 %all-to-all-done.1 = bf16[4,48,1792]{2,1,0:T(8,128)(2,1)S(1)} async-done(((bf16[4,48,1792]{2,1,0:T(8,128)(2,1)}), bf16[4,48,1792]{2,1,0:T(8,128)(2,1)S(1)}, u32[]{:S(2)}, u32[]{:S(2)}) %all-to-all-start.1) | async-done | bytes 688160 | tf_op jit(solution)/shard_map/all_to_all | solution.py:71
  98.5 0.1 convert_reduce_fusion.1
  98.6 0.6 fusion.13
  99.2 0.2 rev.3
  99.5 0.7 all_to_all.18
  100.2 7.8 %all-to-all-start.2 = ((f32[16,1,944]{2,1,0:T(1,128)}), f32[16,1,944]{2,1,0:T(1,128)S(1)}, u32[]{:S(2)}, u32[]{:S(2)}) async-start(f32[16,1,944]{2,1,0:T(1,128)} %all_to_all.18), calls=%async_computation.2 | async-start | bytes 131072 | tf_op jit(solution)/shard_map/all_to_all | solution.py:97
  108.0 6.7 %all-to-all-done.2 = f32[16,1,944]{2,1,0:T(1,128)S(1)} async-done(((f32[16,1,944]{2,1,0:T(1,128)}), f32[16,1,944]{2,1,0:T(1,128)S(1)}, u32[]{:S(2)}, u32[]{:S(2)}) %all-to-all-start.2) | async-done | bytes 60448 | tf_op jit(solution)/shard_map/all_to_all | solution.py:97
  114.8 0.1 reshape.48
  115.0 0.7 broadcast_in_dim.8
  115.7 7.7 %all-to-all-start.3 = ((f32[32,1,1280]{2,1,0:T(1,128)}), f32[32,1,1280]{2,1,0:T(1,128)S(1)}, u32[]{:S(2)}, u32[]{:S(2)}) async-start(f32[32,1,1280]{2,1,0:T(1,128)} %broadcast_in_dim.8), calls=%async_computation.3 | async-start | bytes 327680 | tf_op jit(solution)/shard_map/all_to_all | solution.py:25
  123.4 11.3 %all-to-all-done.3 = f32[32,1,1280]{2,1,0:T(1,128)S(1)} async-done(((f32[32,1,1280]{2,1,0:T(1,128)}), f32[32,1,1280]{2,1,0:T(1,128)S(1)}, u32[]{:S(2)}, u32[]{:S(2)}) %all-to-all-start.3) | async-done | bytes 163872 | tf_op jit(solution)/shard_map/all_to_all | solution.py:25
  134.8 0.4 reduce.2
  135.3 0.6 broadcast_multiply_fusion.1
  135.9 0.6 broadcast_multiply_fusion
  (28 shorter events, 0.4 us)
Async XLA Ops:
  0.6 1.3 copy-start
  3.2 4.3 %collective-permute-start.1 = (f16[192,2048]{1,0:T(8,128)(2,1)S(1)}, f16[192,2048]{1,0:T(8,128)(2,1)S(1)}, u32[]{:S(2)}, u32[]{:S(2)}) collective-permute-start(f16[192,2048]{1,0:T(8,128)(2,1)S(1)} %fusion), channel_id=1, source_target_pairs={{0,16},{16,0},{1,17},{17,1},{2,18},{18,2},{3,19},{19,3},{4,20},{20... | collective-permute-start | bytes 2359304 | tf_op jit(solution)/shard_map/ppermute | solution.py:21
  5.1 73.9 %collective-permute-start.3 = (bf16[896,2048]{1,0:T(8,128)(2,1)}, bf16[896,2048]{1,0:T(8,128)(2,1)S(1)}, u32[]{:S(2)}, u32[]{:S(2)}) collective-permute-start(bf16[896,2048]{1,0:T(8,128)(2,1)} %param.9), channel_id=1, source_target_pairs={{0,16},{16,0},{1,17},{17,1},{2,18},{18,2},{3,19},{19,3},{4,20},{20... | collective-permute-start | bytes 11010056 | tf_op jit(solution)/shard_map/ppermute | solution.py:21
  8.0 71.0 %copy-start.4 = (bf16[896,2048]{1,0:T(8,128)(2,1)S(1)}, bf16[896,2048]{1,0:T(8,128)(2,1)}, u32[]{:S(2)}) copy-start(bf16[896,2048]{1,0:T(8,128)(2,1)} %param.9) | copy-start | bytes 11010052
  41.0 11.6 %collective-permute-start.2 = (f16[24,2048]{1,0:T(8,128)(2,1)S(1)}, f16[24,2048]{1,0:T(8,128)(2,1)S(1)}, u32[]{:S(2)}, u32[]{:S(2)}) collective-permute-start(f16[24,2048]{1,0:T(8,128)(2,1)S(1)} %multiply_convert_fusion.1), channel_id=1, source_target_pairs={{0,32},{32,0},{1,33},{33,1},{2,34},{34,2},{3,35},{35,3},{4,36},{36... | collective-permute-start | bytes 294920 | tf_op jit(solution)/shard_map/ppermute | solution.py:21
  81.7 6.1 %copy-start.1 = (s32[896]{0:T(1024)S(1)}, s32[896]{0:T(1024)}, u32[]{:S(2)}) copy-start(s32[896]{0:T(1024)} %param.13) | copy-start | bytes 10756
  81.7 6.1 %copy-start.2 = (s32[896]{0:T(1024)S(1)}, s32[896]{0:T(1024)}, u32[]{:S(2)}) copy-start(s32[896]{0:T(1024)} %param.11) | copy-start | bytes 10756
  81.7 8.0 %copy-start.3 = (s32[256,2]{0,1:T(2,128)S(1)}, s32[256,2]{0,1:T(2,128)}, u32[]{:S(2)}) copy-start(s32[256,2]{0,1:T(2,128)} %param.12) | copy-start | bytes 6148
  82.7 15.9 %all-to-all-start.1 = ((bf16[4,48,1792]{2,1,0:T(8,128)(2,1)}), bf16[4,48,1792]{2,1,0:T(8,128)(2,1)S(1)}, u32[]{:S(2)}, u32[]{:S(2)}) async-start(bf16[4,48,1792]{2,1,0:T(8,128)(2,1)} %bitcast.3), calls=%async_computation.1 | async-start | bytes 1376256 | tf_op jit(solution)/shard_map/all_to_all | solution.py:71
  87.8 3.1 %collective-permute-start = (s32[2,896]{1,0:T(2,128)S(1)}, s32[2,896]{1,0:T(2,128)S(1)}, u32[]{:S(2)}, u32[]{:S(2)}) collective-permute-start(s32[2,896]{1,0:T(2,128)S(1)} %pad_add_fusion.1), channel_id=1, source_target_pairs={{0,16},{16,0},{1,17},{17,1},{2,18},{18,2},{3,19},{19,3},{4,20},{20... | collective-permute-start | bytes 21512 | tf_op jit(solution)/shard_map/ppermute | solution.py:21
  100.2 14.6 %all-to-all-start.2 = ((f32[16,1,944]{2,1,0:T(1,128)}), f32[16,1,944]{2,1,0:T(1,128)S(1)}, u32[]{:S(2)}, u32[]{:S(2)}) async-start(f32[16,1,944]{2,1,0:T(1,128)} %all_to_all.18), calls=%async_computation.2 | async-start | bytes 131072 | tf_op jit(solution)/shard_map/all_to_all | solution.py:97
  115.7 19.1 %all-to-all-start.3 = ((f32[32,1,1280]{2,1,0:T(1,128)}), f32[32,1,1280]{2,1,0:T(1,128)S(1)}, u32[]{:S(2)}, u32[]{:S(2)}) async-start(f32[32,1,1280]{2,1,0:T(1,128)} %broadcast_in_dim.8), calls=%async_computation.3 | async-start | bytes 327680 | tf_op jit(solution)/shard_map/all_to_all | solution.py:25
